TPU v7x, 256 devices: a whole 4x4x8 slice. The times are simulated.
256 devices in a mesh: wide: 64 (over y, x, z_hi), narrow: 4 (over z_lo, core).
Axes of the slice: x: 4, y: 4, z: 8 (z_hi: 4, z_lo: 2; z = z_hi * 2 + z_lo), core: 2. Of those that a mesh axis runs over, the one named last changes fastest.
Arguments:
- target_position: float32 [3, 16384], P(None, ('wide', 'narrow')), may hold values from 0 to 4
- target_vector: float32 [3, 16384], P(None, ('wide', 'narrow')), may hold values from -4 to 4
- target_radius: float32 [16384], P(('wide', 'narrow')), may hold values from 0.05 to 0.5
- source_position: float32 [3, 262144], P(None, ('wide', 'narrow')), may hold values from 0 to 4
- source_vector: float32 [3, 262144], P(None, ('wide', 'narrow')), may hold values from -4 to 4
- source_radius: float32 [262144], P(('wide', 'narrow')), may hold values from 0.05 to 0.5
- source_current: float32 [262144], P(('wide', 'narrow')), may hold values from -0.125 to 0.125
- incidence: int32 [262144], P(('wide', 'narrow')), may hold values from 0 to 127
- excitation: int32 [128], replicated, may hold values from 0 to 127, each once
Outputs:
- voltages: float32 [16384, 128], P(('wide', 'narrow'))
Inputs may be any that keep to these rules, and one draw needn't show every extreme that they name: Each excitation column excites a different port.
All inputs are finite; a program needn't handle non-finite values.
Results may differ from a plain program's by a relative error of at most 0.0043.
Values sent between devices are 32-bit elements; how exact they have to be, the bound alone decides.
No kernel may reach another device: no remote copies, remote signals or barrier semaphores. Data moves between devices by JAX's collectives and lax.ppermute only.
A program may use at most 128 MiB of HBM per device.

v0:
```python
import jax
import jax.numpy as jnp
from jax import lax
from jax.experimental import pallas as pl
from jax.experimental.pallas import tpu as pltpu
from jax.sharding import Mesh, PartitionSpec as P

BF16 = jnp.bfloat16
F32 = jnp.float32
DEPTH = 64
LANES = 128
COUNT = 64
WIDTH = 1024
AXES = ("y", "x", "zh", "zl", "c")
SHAPE = (4, 4, 4, 2, 2)
FLIPS = (0, 1, 2, 3)


def split3(x):
    high = x.astype(BF16).astype(F32)
    rest = x - high
    middle = rest.astype(BF16).astype(F32)
    low = (rest - middle).astype(BF16).astype(F32)
    return high, middle, low


def centred(x):
    row = lax.broadcasted_iota(jnp.int32, x.shape, 0)
    x = jnp.where(row < 3, x - 2.0, x)
    norm = jnp.sum(jnp.where(row < 4, x * x, 0.0), axis=0, keepdims=True)
    return row, x, split3(norm)


def source_features(x):
    row, x, (n_high, n_middle, n_low) = centred(x)
    high, middle, low = split3(x)
    norms = jnp.where(
        row == 0,
        n_high,
        jnp.where(row == 1, n_middle, jnp.where(row == 2, n_low, jnp.where(row < 6, 1.0, 0.0))),
    )
    parts = [high, high, high, middle, middle, low, norms, jnp.zeros_like(x)]
    return jnp.concatenate(parts, 0)


def target_features(x):
    row, x, (n_high, n_middle, n_low) = centred(x)
    high, middle, low = split3(x)
    norms = jnp.where(
        row < 3,
        1.0,
        jnp.where(row == 3, n_high, jnp.where(row == 4, n_middle, jnp.where(row == 5, n_low, 0.0))),
    )
    weight = jnp.where(row < 3, -2.0, jnp.where(row == 3, 2.0, 0.0))
    parts = [p * weight for p in (high, middle, low, high, middle, high)]
    return jnp.concatenate(parts + [norms, jnp.zeros_like(x)], 0)


def pack_targets_kernel(position, vector, radius, block):
    count = radius.shape[1]
    rows = [position[...], radius[...], vector[...], jnp.zeros((1, count), F32)]
    wide = [jnp.concatenate(rows, 0), jnp.zeros((8, LANES - count), F32)]
    block[...] = jnp.concatenate(wide, 1)


def pack_sources_kernel(position, vector, radius, current, incidence, excitation, copies, ports):
    sources = copies.at[0]
    for r in range(8):
        here = slice(r * LANES, (r + 1) * LANES)
        for q in range(3):
            sources[8 * q + r : 8 * q + r + 1, :] = position[q : q + 1, here]
            sources[8 * q + r + 32 : 8 * q + r + 33, :] = vector[q : q + 1, here]
    sources[24:32, :] = radius[...]
    sources[56:64, :] = current[...]
    sources[64:72, :] = incidence[...].astype(F32)
    for i in range(1, copies.shape[0]):
        copies[i] = copies[0]
    ports[...] = jnp.transpose(jnp.broadcast_to(excitation[...].astype(F32), ports.shape))


def pack(kernel, name, shapes, *arrays):
    vmem = pl.BlockSpec(memory_space=pltpu.VMEM)
    return pl.pallas_call(
        kernel,
        out_shape=[jax.ShapeDtypeStruct(shape, F32) for shape in shapes],
        in_specs=[vmem] * len(arrays),
        out_specs=[vmem] * len(shapes),
        name=name,
    )(*arrays)


def prepare_targets(pairs, squared, vectors):
    for j in range(2 * len(FLIPS)):
        here = slice(j * COUNT, (j + 1) * COUNT)
        x = pairs[j % len(FLIPS)][j // len(FLIPS)]
        squared[here, :] = jnp.transpose(target_features(x))[:COUNT].astype(BF16)
        for d in range(3):
            spread = jnp.broadcast_to(x[4 + d : 5 + d, :], (LANES, LANES))
            vectors[d, here, :] = jnp.transpose(spread)[:COUNT]


def add_sources(sources, ports, squared, vectors, total, even, odd):
    port = ports[...]
    blocks = sources.shape[0]

    def prepare(b, features, raw, currents):
        for r in range(WIDTH // LANES):
            here = slice(r * LANES, (r + 1) * LANES)
            x = sources[b, pl.ds(r, 8, stride=8), :]
            features[:, here] = source_features(x).astype(BF16)
            raw[:, here] = x
            current = sources[b, pl.ds(56 + r, 1), :]
            incidence = sources[b, pl.ds(64 + r, 1), :]
            matched = jnp.where(port == incidence, current, 0.0)
            currents[here, :] = jnp.transpose(matched).astype(BF16)

    def add(features, raw, currents):
        step = 256
        for s in range(0, WIDTH, step):
            these = slice(s, s + step)
            distance = jnp.dot(squared[...], features[:, these], preferred_element_type=F32)
            alignment = []
            for t in range(s, s + step, LANES):
                here = slice(t, t + LANES)
                alignment.append(
                    vectors[0] * raw[4:5, here]
                    + vectors[1] * raw[5:6, here]
                    + vectors[2] * raw[6:7, here]
                )
            inductance = jnp.concatenate(alignment, 1) * lax.rsqrt(distance)
            total[...] += jnp.dot(
                inductance.astype(BF16), currents[these, :], preferred_element_type=F32
            )

    prepare(0, *even)

    def two(i, carry):
        prepare(2 * i + 1, *odd)
        add(*even)
        prepare(jnp.minimum(2 * i + 2, blocks - 1), *even)
        add(*odd)
        return carry

    lax.fori_loop(0, blocks // 2, two, 0)


def near_kernel(*refs):
    pairs, refs = refs[: len(FLIPS)], refs[len(FLIPS) :]
    sources, ports, squared, vectors, total, *buffers = refs
    prepare_targets(pairs, squared, vectors)
    total[...] = jnp.zeros_like(total)
    add_sources(sources, ports, squared, vectors, total, buffers[:3], buffers[3:])


def far_kernel(sources, ports, squared, vectors, start, keep, send, total, *buffers):
    total[...] = start[...]
    add_sources(sources, ports, squared, vectors, total, buffers[:3], buffers[3:])
    half = total.shape[0] // 2
    keep[...] = total[:half, :]
    send[...] = total[half:, :]


ROWS = 2 * len(FLIPS) * COUNT
BUFFERS = [
    pltpu.VMEM((DEPTH, WIDTH), BF16),
    pltpu.VMEM((8, WIDTH), F32),
    pltpu.VMEM((WIDTH, LANES), BF16),
] * 2


def options(sources):
    pairs = ROWS * sources.shape[0] * WIDTH
    return {
        "compiler_params": pltpu.CompilerParams(vmem_limit_bytes=24 * 2**20),
        "cost_estimate": pl.CostEstimate(
            flops=2 * pairs * (DEPTH + LANES), bytes_accessed=2**21, transcendentals=pairs
        ),
    }


def near_volts(pairs, sources, ports):
    vmem = pl.BlockSpec(memory_space=pltpu.VMEM)
    return pl.pallas_call(
        near_kernel,
        out_shape=[
            jax.ShapeDtypeStruct((ROWS, DEPTH), BF16),
            jax.ShapeDtypeStruct((3, ROWS, LANES), F32),
            jax.ShapeDtypeStruct((ROWS, LANES), F32),
        ],
        in_specs=[vmem] * (len(FLIPS) + 2),
        out_specs=[vmem] * 3,
        scratch_shapes=BUFFERS,
        name="near_volts",
        **options(sources),
    )(*pairs, sources, ports)


def far_volts(sources, ports, squared, vectors, start):
    vmem = pl.BlockSpec(memory_space=pltpu.VMEM)
    return pl.pallas_call(
        far_kernel,
        out_shape=[jax.ShapeDtypeStruct((ROWS // 2, LANES), F32)] * 2,
        in_specs=[vmem] * 5,
        out_specs=[vmem] * 2,
        scratch_shapes=[pltpu.VMEM((ROWS, LANES), F32)] + BUFFERS,
        name="far_volts",
        **options(sources),
    )(sources, ports, squared, vectors, start)


def per_device(
    target_position,
    target_vector,
    target_radius,
    source_position,
    source_vector,
    source_radius,
    source_current,
    incidence,
    excitation,
):
    plane = SHAPE[0] * SHAPE[1]
    (block,) = pack(
        pack_targets_kernel,
        "pack_targets",
        [(8, LANES)],
        target_position,
        target_vector,
        target_radius[None],
    )
    swap = [(0, 1), (1, 0)]
    other = lax.ppermute(block, "c", swap)
    copies, ports = pack(
        pack_sources_kernel,
        "pack_sources",
        [(plane, 72, LANES), (LANES, LANES)],
        source_position,
        source_vector,
        source_radius.reshape(8, LANES),
        source_current.reshape(8, LANES),
        incidence.reshape(8, LANES),
        excitation[None],
    )
    copies, other = lax.optimization_barrier((copies, other))
    sources = lax.all_to_all(copies, ("y", "x"), 0, 0, tiled=True)
    pair = jnp.stack([block, other])
    zh = range(SHAPE[2])
    pairs = [pair] + [lax.ppermute(pair, "zh", [(i, i ^ k) for i in zh]) for k in FLIPS[1:]]
    sources, pairs = lax.optimization_barrier((sources, pairs))
    far = lax.ppermute(sources, "zl", swap)
    prepared = near_volts(pairs, sources, ports)
    keep, send = far_volts(far, ports, *prepared)
    partial = (keep + lax.ppermute(send, "c", swap)).reshape(len(FLIPS), COUNT, LANES)
    shares = [partial[0]]
    shares += [lax.ppermute(partial[k], "zh", [(i, i ^ k) for i in zh]) for k in FLIPS[1:]]
    return sum(shares[1:], shares[0])


def solution(mesh):
    fine = Mesh(mesh.devices.reshape(SHAPE), AXES)
    placed = (P(None, AXES), P(None, AXES), P(AXES), P(None, AXES), P(None, AXES))
    placed += (P(AXES), P(AXES), P(AXES), P())
    return jax.shard_map(
        per_device, mesh=fine, in_specs=placed, out_specs=P(AXES, None), check_vma=False
    )
```

profile of v0, /device:TPU:32, one launch (start us, length us, event | category | flops | bytes accessed | tf_op | source)
XLA Modules:
  0.0 65.4 jit_solution(2703897899444509462)
XLA Ops:
  0.0 1.3 %pack_targets.1 = f32[8,128]{1,0:T(8,128)} custom-call(f32[3,64]{1,0:T(4,128)} %position.3, f32[3,64]{1,0:T(4,128)} %vector.3, f32[1,64]{1,0:T(1,128)} %bitcast.13), custom_call_target="tpu_custom_call" | custom-call | tf_op jit(solution)/shard_map/pack_targets/pallas_call | solution.py:83
  1.3 0.0 collective-permute-start
  1.3 1.7 %pack_sources.1 = (f32[16,72,128]{2,1,0:T(8,128)}, f32[128,128]{1,0:T(8,128)}) custom-call(f32[3,1024]{1,0:T(4,128)} %position.2, f32[3,1024]{1,0:T(4,128)} %vector.2, f32[8,128]{1,0:T(8,128)} %bitcast.8, f32[8,128]{1,0:T(8,128)} %bitcast.9, s32[8,128]{1,0:T(8,128)} %bitcast.10, s32[1,128]{1,0:T(1,128)} %bitcast.12), custom_call_target="tpu_custom_call" | custom-call | tf_op jit(solution)/shard_map/pack_sources/pallas_call | solution.py:83
  3.0 0.0 collective-permute-done
  3.0 0.0 copy-start.1
  3.0 0.0 copy-start
  3.0 7.2 %all-to-all-start = ((f32[16,72,128]{2,1,0:T(8,128)}), f32[16,72,128]{2,1,0:T(8,128)S(1)}, u32[]{:S(2)}, u32[]{:S(2)}) async-start(f32[16,72,128]{2,1,0:T(8,128)} %get-tuple-element.20), calls=%async_computation | async-start | bytes 1179648 | tf_op jit(solution)/shard_map/all_to_all | solution.py:245
  10.2 0.0 copy-done.1
  10.2 3.4 %collective-permute-start.1 = (f32[2,8,128]{2,1,0:T(8,128)S(1)}, f32[2,8,128]{2,1,0:T(8,128)S(1)}, u32[]{:S(2)}, u32[]{:S(2)}) collective-permute-start(f32[2,8,128]{2,1,0:T(8,128)S(1)} %pad_maximum_fusion.refs_0_), channel_id=1, source_target_pairs={{0,4},{4,0},{8,12},{12,8},{1,5},{5,1},{9,13},{13,9},{2,6},{6,2},{1... | collective-permute-start | bytes 24584 | tf_op jit(solution)/shard_map/ppermute | solution.py:248
  13.5 4.5 %collective-permute-start.2 = (f32[2,8,128]{2,1,0:T(8,128)S(1)}, f32[2,8,128]{2,1,0:T(8,128)S(1)}, u32[]{:S(2)}, u32[]{:S(2)}) collective-permute-start(f32[2,8,128]{2,1,0:T(8,128)S(1)} %pad_maximum_fusion.refs_0_), channel_id=1, source_target_pairs={{0,8},{4,12},{8,0},{12,4},{1,9},{5,13},{9,1},{13,5},{2,10},{6,14},... | collective-permute-start | bytes 24584 | tf_op jit(solution)/shard_map/ppermute | solution.py:248
  18.0 0.0 collective-permute-start.3
  18.0 0.0 collective-permute-done.1.refs_1_
  18.0 3.1 %collective-permute-done.2.refs_2_ = f32[2,8,128]{2,1,0:T(8,128)S(1)} collective-permute-done((f32[2,8,128]{2,1,0:T(8,128)S(1)}, f32[2,8,128]{2,1,0:T(8,128)S(1)}, u32[]{:S(2)}, u32[]{:S(2)}) %collective-permute-start.2) | collective-permute-done | bytes 8224 | tf_op jit(solution)/shard_map/ppermute | solution.py:248
  21.1 2.7 %collective-permute-done.3.refs_3_ = f32[2,8,128]{2,1,0:T(8,128)S(1)} collective-permute-done((f32[2,8,128]{2,1,0:T(8,128)S(1)}, f32[2,8,128]{2,1,0:T(8,128)S(1)}, u32[]{:S(2)}, u32[]{:S(2)}) %collective-permute-start.3) | collective-permute-done | bytes 8224 | tf_op jit(solution)/shard_map/ppermute | solution.py:248
  23.8 0.0 all-to-all-done.refs_4_
  23.8 1.0 %collective-permute-start.4 = (f32[16,72,128]{2,1,0:T(8,128)S(1)}, f32[16,72,128]{2,1,0:T(8,128)S(1)}, u32[]{:S(2)}, u32[]{:S(2)}) collective-permute-start(f32[16,72,128]{2,1,0:T(8,128)S(1)} %all-to-all-done.refs_4_), channel_id=1, source_target_pairs={{0,2},{2,0},{1,3},{3,1},{4,6},{6,4},{5,7},{7,5},{8,10},{10,8},{9,1... | collective-permute-start | bytes 1769480 | tf_op jit(solution)/shard_map/ppermute | solution.py:250
  24.8 0.0 copy-done
  24.8 12.4 %near_volts.1 = (bf16[512,64]{1,0:T(8,128)(2,1)S(1)}, f32[3,512,128]{2,1,0:T(8,128)S(1)}, f32[512,128]{1,0:T(8,128)S(1)}) custom-call(f32[2,8,128]{2,1,0:T(8,128)S(1)} %pad_maximum_fusion.refs_0_, f32[2,8,128]{2,1,0:T(8,128)S(1)} %collective-permute-done.1.refs_1_, f32[2,8,128]{2,1,0:T(8,128)S(1)} %collective-permute-done.2.refs_2_, ...), custom_call_target="tpu_custom_call" | custom-call | flops 3221225472 | bytes 2097152 | tf_op jit(solution)/shard_map/near_volts/pallas_call | solution.py:183
  37.2 0.6 collective-permute-done.4.sources
  37.8 12.0 %far_volts.1 = (f32[256,128]{1,0:T(8,128)S(1)}, f32[256,128]{1,0:T(8,128)S(1)}) custom-call(f32[16,72,128]{2,1,0:T(8,128)S(1)} %collective-permute-done.4.sources, f32[128,128]{1,0:T(8,128)S(1)} %copy-done, bf16[512,64]{1,0:T(8,128)(2,1)S(1)} %get-tuple-element.28.squared, f32[3,512,128]{2,1,0:T(8,128)S(1)} %get-tuple-element.29.vectors, ...), custom_call_target="tpu_custom_call" | custom-call | flops 3221225472 | bytes 2097152 | tf_op jit(solution)/shard_map/far_volts/pallas_call | solution.py:200
  49.8 0.1 collective-permute-start.5
  49.9 1.3 %collective-permute-done.5 = f32[256,128]{1,0:T(8,128)S(1)} collective-permute-done((f32[256,128]{1,0:T(8,128)S(1)}, f32[256,128]{1,0:T(8,128)S(1)}, u32[]{:S(2)}, u32[]{:S(2)}) %collective-permute-start.5) | collective-permute-done | bytes 131104 | tf_op jit(solution)/shard_map/ppermute | solution.py:253
  51.3 2.9 %collective-permute-start.6 = (f32[64,128]{1,0:T(8,128)S(1)}, f32[64,128]{1,0:T(8,128)S(1)}, u32[]{:S(2)}, u32[]{:S(2)}) collective-permute-start(f32[64,128]{1,0:T(8,128)S(1)} %get-tuple-element.33), channel_id=1, source_target_pairs={{0,4},{4,0},{8,12},{12,8},{1,5},{5,1},{9,13},{13,9},{2,6},{6,2},{1... | collective-permute-start | bytes 98312 | tf_op jit(solution)/shard_map/ppermute | solution.py:255
  54.2 4.5 %collective-permute-start.7 = (f32[64,128]{1,0:T(8,128)S(1)}, f32[64,128]{1,0:T(8,128)S(1)}, u32[]{:S(2)}, u32[]{:S(2)}) collective-permute-start(f32[64,128]{1,0:T(8,128)S(1)} %get-tuple-element.35), channel_id=1, source_target_pairs={{0,8},{4,12},{8,0},{12,4},{1,9},{5,13},{9,1},{13,5},{2,10},{6,14},... | collective-permute-start | bytes 98312 | tf_op jit(solution)/shard_map/ppermute | solution.py:255
  58.7 0.0 collective-permute-start.8
  58.7 0.0 collective-permute-done.6
  58.7 3.7 %collective-permute-done.7 = f32[64,128]{1,0:T(8,128)S(1)} collective-permute-done((f32[64,128]{1,0:T(8,128)S(1)}, f32[64,128]{1,0:T(8,128)S(1)}, u32[]{:S(2)}, u32[]{:S(2)}) %collective-permute-start.7) | collective-permute-done | bytes 32800 | tf_op jit(solution)/shard_map/ppermute | solution.py:255
  62.4 2.3 %collective-permute-done.8 = f32[64,128]{1,0:T(8,128)S(1)} collective-permute-done((f32[64,128]{1,0:T(8,128)S(1)}, f32[64,128]{1,0:T(8,128)S(1)}, u32[]{:S(2)}, u32[]{:S(2)}) %collective-permute-start.8) | collective-permute-done | bytes 32800 | tf_op jit(solution)/shard_map/ppermute | solution.py:255
  64.7 0.6 fusion.1
  (3 shorter events, 0.0 us)
Async XLA Ops:
  1.3 1.7 %collective-permute-start = (f32[8,128]{1,0:T(8,128)}, f32[8,128]{1,0:T(8,128)S(1)}, u32[]{:S(2)}, u32[]{:S(2)}) collective-permute-start(f32[8,128]{1,0:T(8,128)} %pack_targets.1), channel_id=1, source_target_pairs={{0,1},{1,0},{2,3},{3,2},{4,5},{5,4},{6,7},{7,6},{8,9},{9,8},{10,11... | collective-permute-start | bytes 12296 | tf_op jit(solution)/shard_map/ppermute | solution.py:232
  3.0 7.2 %copy-start.1 = (f32[8,128]{1,0:T(8,128)S(1)}, f32[8,128]{1,0:T(8,128)}, u32[]{:S(2)}) copy-start(f32[8,128]{1,0:T(8,128)} %pack_targets.1) | copy-start | bytes 12292
  3.0 21.8 %copy-start = (f32[128,128]{1,0:T(8,128)S(1)}, f32[128,128]{1,0:T(8,128)}, u32[]{:S(2)}) copy-start(f32[128,128]{1,0:T(8,128)} %get-tuple-element.23.refs_5_.ports) | copy-start | bytes 196612
  3.0 20.8 %all-to-all-start = ((f32[16,72,128]{2,1,0:T(8,128)}), f32[16,72,128]{2,1,0:T(8,128)S(1)}, u32[]{:S(2)}, u32[]{:S(2)}) async-start(f32[16,72,128]{2,1,0:T(8,128)} %get-tuple-element.20), calls=%async_computation | async-start | bytes 1179648 | tf_op jit(solution)/shard_map/all_to_all | solution.py:245
  10.2 7.9 %collective-permute-start.1 = (f32[2,8,128]{2,1,0:T(8,128)S(1)}, f32[2,8,128]{2,1,0:T(8,128)S(1)}, u32[]{:S(2)}, u32[]{:S(2)}) collective-permute-start(f32[2,8,128]{2,1,0:T(8,128)S(1)} %pad_maximum_fusion.refs_0_), channel_id=1, source_target_pairs={{0,4},{4,0},{8,12},{12,8},{1,5},{5,1},{9,13},{13,9},{2,6},{6,2},{1... | collective-permute-start | bytes 24584 | tf_op jit(solution)/shard_map/ppermute | solution.py:248
  13.5 7.6 %collective-permute-start.2 = (f32[2,8,128]{2,1,0:T(8,128)S(1)}, f32[2,8,128]{2,1,0:T(8,128)S(1)}, u32[]{:S(2)}, u32[]{:S(2)}) collective-permute-start(f32[2,8,128]{2,1,0:T(8,128)S(1)} %pad_maximum_fusion.refs_0_), channel_id=1, source_target_pairs={{0,8},{4,12},{8,0},{12,4},{1,9},{5,13},{9,1},{13,5},{2,10},{6,14},... | collective-permute-start | bytes 24584 | tf_op jit(solution)/shard_map/ppermute | solution.py:248
  18.0 5.8 %collective-permute-start.3 = (f32[2,8,128]{2,1,0:T(8,128)S(1)}, f32[2,8,128]{2,1,0:T(8,128)S(1)}, u32[]{:S(2)}, u32[]{:S(2)}) collective-permute-start(f32[2,8,128]{2,1,0:T(8,128)S(1)} %pad_maximum_fusion.refs_0_), channel_id=1, source_target_pairs={{0,12},{4,8},{8,4},{12,0},{1,13},{5,9},{9,5},{13,1},{2,14},{6,10},... | collective-permute-start | bytes 24584 | tf_op jit(solution)/shard_map/ppermute | solution.py:248
  23.8 14.0 %collective-permute-start.4 = (f32[16,72,128]{2,1,0:T(8,128)S(1)}, f32[16,72,128]{2,1,0:T(8,128)S(1)}, u32[]{:S(2)}, u32[]{:S(2)}) collective-permute-start(f32[16,72,128]{2,1,0:T(8,128)S(1)} %all-to-all-done.refs_4_), channel_id=1, source_target_pairs={{0,2},{2,0},{1,3},{3,1},{4,6},{6,4},{5,7},{7,5},{8,10},{10,8},{9,1... | collective-permute-start | bytes 1769480 | tf_op jit(solution)/shard_map/ppermute | solution.py:250
  49.8 1.4 %collective-permute-start.5 = (f32[256,128]{1,0:T(8,128)S(1)}, f32[256,128]{1,0:T(8,128)S(1)}, u32[]{:S(2)}, u32[]{:S(2)}) collective-permute-start(f32[256,128]{1,0:T(8,128)S(1)} %get-tuple-element.32), channel_id=1, source_target_pairs={{0,1},{1,0},{2,3},{3,2},{4,5},{5,4},{6,7},{7,6},{8,9},{9,8},{10,11... | collective-permute-start | bytes 393224 | tf_op jit(solution)/shard_map/ppermute | solution.py:253
  51.3 7.4 %collective-permute-start.6 = (f32[64,128]{1,0:T(8,128)S(1)}, f32[64,128]{1,0:T(8,128)S(1)}, u32[]{:S(2)}, u32[]{:S(2)}) collective-permute-start(f32[64,128]{1,0:T(8,128)S(1)} %get-tuple-element.33), channel_id=1, source_target_pairs={{0,4},{4,0},{8,12},{12,8},{1,5},{5,1},{9,13},{13,9},{2,6},{6,2},{1... | collective-permute-start | bytes 98312 | tf_op jit(solution)/shard_map/ppermute | solution.py:255
  54.2 8.2 %collective-permute-start.7 = (f32[64,128]{1,0:T(8,128)S(1)}, f32[64,128]{1,0:T(8,128)S(1)}, u32[]{:S(2)}, u32[]{:S(2)}) collective-permute-start(f32[64,128]{1,0:T(8,128)S(1)} %get-tuple-element.35), channel_id=1, source_target_pairs={{0,8},{4,12},{8,0},{12,4},{1,9},{5,13},{9,1},{13,5},{2,10},{6,14},... | collective-permute-start | bytes 98312 | tf_op jit(solution)/shard_map/ppermute | solution.py:255
  58.7 6.0 %collective-permute-start.8 = (f32[64,128]{1,0:T(8,128)S(1)}, f32[64,128]{1,0:T(8,128)S(1)}, u32[]{:S(2)}, u32[]{:S(2)}) collective-permute-start(f32[64,128]{1,0:T(8,128)S(1)} %get-tuple-element.34), channel_id=1, source_target_pairs={{0,12},{4,8},{8,4},{12,0},{1,13},{5,9},{9,5},{13,1},{2,14},{6,10},... | collective-permute-start | bytes 98312 | tf_op jit(solution)/shard_map/ppermute | solution.py:255
where the time goes:
time: 66 us; the launch traced here: 65.4 us
  Pallas kernels  27.3 us (41%)
  starting transfers between devices  23.6 us (36%)
  waiting for transfers between devices  13.7 us (21%)
    pallas_call x1, Pallas kernels, near_volts(): pl.pallas_call(near_kernel, out_shape=[jax.ShapeDtypeStruct((ROWS, DEPTH)...  12.4 us
    pallas_call x1, Pallas kernels, far_volts(): pl.pallas_call(far_kernel, out_shape=[jax.ShapeDtypeStruct((ROWS // 2, LA...  12 us
    ppermute x3, starting transfers between devices, per_device(): lax.ppermute(pair, 'zh', [(i, i ^ k) for i in zh])  7.85 us
    ppermute x3, starting transfers between devices, per_device(): lax.ppermute(partial[k], 'zh', [(i, i ^ k) for i in zh])  7.42 us
    all_to_all x1, starting transfers between devices, per_device(): sources = lax.all_to_all(copies, ('y', 'x'), 0, 0, tiled=True)  7.18 us
    ppermute x3, waiting for transfers between devices, per_device(): lax.ppermute(partial[k], 'zh', [(i, i ^ k) for i in zh])  6.02 us
    ppermute x3, waiting for transfers between devices, per_device(): lax.ppermute(pair, 'zh', [(i, i ^ k) for i in zh])  5.76 us
    pallas_call x2, Pallas kernels, pack(): pl.pallas_call(kernel, out_shape=[jax.ShapeDtypeStruct(shape, F32) for sh...  2.96 us
  transfers between devices with their start and end apart: 10, of which 6 were waited for; matrix products, arithmetic and copies ran while one was open for 0% of the time, Pallas kernels for 22%

commit v1 on v0

--- a/solution.py
+++ b/solution.py
@@ -13,7 +13,7 @@
 WIDTH = 1024
 AXES = ("y", "x", "zh", "zl", "c")
 SHAPE = (4, 4, 4, 2, 2)
-FLIPS = (0, 1, 2, 3)
+FLIPS = (0, 2, 1, 3)
 
 
 def split3(x):
@@ -56,14 +56,12 @@
     return jnp.concatenate(parts + [norms, jnp.zeros_like(x)], 0)
 
 
-def pack_targets_kernel(position, vector, radius, block):
-    count = radius.shape[1]
-    rows = [position[...], radius[...], vector[...], jnp.zeros((1, count), F32)]
+def pack_kernel(t_position, t_vector, t_radius, *refs):
+    position, vector, radius, current, incidence, excitation, block, copies, ports = refs
+    count = t_radius.shape[1]
+    rows = [t_position[...], t_radius[...], t_vector[...], jnp.zeros((1, count), F32)]
     wide = [jnp.concatenate(rows, 0), jnp.zeros((8, LANES - count), F32)]
     block[...] = jnp.concatenate(wide, 1)
-
-
-def pack_sources_kernel(position, vector, radius, current, incidence, excitation, copies, ports):
     sources = copies.at[0]
     for r in range(8):
         here = slice(r * LANES, (r + 1) * LANES)
@@ -78,14 +76,14 @@
     ports[...] = jnp.transpose(jnp.broadcast_to(excitation[...].astype(F32), ports.shape))
 
 
-def pack(kernel, name, shapes, *arrays):
+def pack(shapes, *arrays):
     vmem = pl.BlockSpec(memory_space=pltpu.VMEM)
     return pl.pallas_call(
-        kernel,
+        pack_kernel,
         out_shape=[jax.ShapeDtypeStruct(shape, F32) for shape in shapes],
         in_specs=[vmem] * len(arrays),
         out_specs=[vmem] * len(shapes),
-        name=name,
+        name="pack",
     )(*arrays)
 
 
@@ -220,20 +218,11 @@
     excitation,
 ):
     plane = SHAPE[0] * SHAPE[1]
-    (block,) = pack(
-        pack_targets_kernel,
-        "pack_targets",
-        [(8, LANES)],
+    block, copies, ports = pack(
+        [(8, LANES), (plane, 72, LANES), (LANES, LANES)],
         target_position,
         target_vector,
         target_radius[None],
-    )
-    swap = [(0, 1), (1, 0)]
-    other = lax.ppermute(block, "c", swap)
-    copies, ports = pack(
-        pack_sources_kernel,
-        "pack_sources",
-        [(plane, 72, LANES), (LANES, LANES)],
         source_position,
         source_vector,
         source_radius.reshape(8, LANES),
@@ -241,7 +230,8 @@
         incidence.reshape(8, LANES),
         excitation[None],
     )
-    copies, other = lax.optimization_barrier((copies, other))
+    swap = [(0, 1), (1, 0)]
+    other = lax.ppermute(block, "c", swap)
     sources = lax.all_to_all(copies, ("y", "x"), 0, 0, tiled=True)
     pair = jnp.stack([block, other])
     zh = range(SHAPE[2])
@@ -252,7 +242,8 @@
     keep, send = far_volts(far, ports, *prepared)
     partial = (keep + lax.ppermute(send, "c", swap)).reshape(len(FLIPS), COUNT, LANES)
     shares = [partial[0]]
-    shares += [lax.ppermute(partial[k], "zh", [(i, i ^ k) for i in zh]) for k in FLIPS[1:]]
+    for j, k in enumerate(FLIPS[1:], 1):
+        shares.append(lax.ppermute(partial[j], "zh", [(i, i ^ k) for i in zh]))
     return sum(shares[1:], shares[0])
 
 

time: 66 us -> 63.3 us (0.959)
  Pallas kernels: 27.3 us -> 26.1 us
  starting transfers between devices: 23.6 us -> 22.7 us
    ppermute x3, waiting for transfers between devices: 6.02 us -> 4.66 us  [per_device(): shares.append(lax.ppermute(partial[j], 'zh', [(i, i ^ k) for i in zh]))]
    pallas_call x2 -> x1, Pallas kernels: 2.96 us -> 1.7 us  [pack(): pl.pallas_call(pack_kernel, out_shape=[jax.ShapeDtypeStruct(shape, F32) f...]
    ppermute x1, waiting for transfers between devices: 0.01 us -> 1.15 us  [per_device(): other = lax.ppermute(block, 'c', swap)]
    ppermute x3, starting transfers between devices: 7.42 us -> 6.58 us  [per_device(): shares.append(lax.ppermute(partial[j], 'zh', [(i, i ^ k) for i in zh]))]
  transfers between devices with their start and end apart: 10 -> 10, of which waited for: 6 -> 9; matrix products, arithmetic and copies ran while one was open for 0% -> 0% of each run, Pallas kernels for 22% -> 20%
where the time goes in v1:
time: 63.3 us; the launch traced here: 62.7 us
  Pallas kernels  26.1 us (41%)
  starting transfers between devices  22.7 us (36%)
  waiting for transfers between devices  13.2 us (21%)
  other arithmetic  0.64 us (1%)
    pallas_call x1, Pallas kernels, near_volts(): pl.pallas_call(near_kernel, out_shape=[jax.ShapeDtypeStruct((ROWS, DEPTH)...  12.4 us
    pallas_call x1, Pallas kernels, far_volts(): pl.pallas_call(far_kernel, out_shape=[jax.ShapeDtypeStruct((ROWS // 2, LA...  12 us
    ppermute x3, starting transfers between devices, per_device(): lax.ppermute(pair, 'zh', [(i, i ^ k) for i in zh])  7.77 us
    all_to_all x1, starting transfers between devices, per_device(): sources = lax.all_to_all(copies, ('y', 'x'), 0, 0, tiled=True)  7.17 us
    ppermute x3, starting transfers between devices, per_device(): shares.append(lax.ppermute(partial[j], 'zh', [(i, i ^ k) for i in zh]))  6.58 us
    ppermute x3, waiting for transfers between devices, per_device(): lax.ppermute(pair, 'zh', [(i, i ^ k) for i in zh])  5.76 us
    ppermute x3, waiting for transfers between devices, per_device(): shares.append(lax.ppermute(partial[j], 'zh', [(i, i ^ k) for i in zh]))  4.66 us
    pallas_call x1, Pallas kernels, pack(): pl.pallas_call(pack_kernel, out_shape=[jax.ShapeDtypeStruct(shape, F32) f...  1.7 us
  transfers between devices with their start and end apart: 10, of which 9 were waited for; matrix products, arithmetic and copies ran while one was open for 0% of the time, Pallas kernels for 20%

profile of v1, /device:TPU:32, one launch (start us, length us, event | category | flops | bytes accessed | tf_op | source)
XLA Modules:
  0.0 62.7 jit_solution(3583439014732133691)
XLA Ops:
  0.0 1.7 %pack.1 = (f32[8,128]{1,0:T(8,128)}, f32[16,72,128]{2,1,0:T(8,128)}, f32[128,128]{1,0:T(8,128)}) custom-call(f32[3,64]{1,0:T(4,128)} %t_position.1, f32[3,64]{1,0:T(4,128)} %t_vector.1, f32[1,64]{1,0:T(1,128)} %bitcast.12, f32[3,1024]{1,0:T(4,128)} %refs_0_.1, f32[3,1024]{1,0:T(4,128)} %refs_1_.1, f32[8,128]{1,0:T(8,128)} %bitcast.7, f32[8,128]{1,0:T(8,128)} %bitcast.8, ...), custom_call_target="tpu_custom_call" | custom-call | tf_op jit(solution)/shard_map/pack/pallas_call | solution.py:81
  1.7 0.0 copy-start.1
  1.7 0.0 copy-start
  1.7 7.2 %all-to-all-start = ((f32[16,72,128]{2,1,0:T(8,128)}), f32[16,72,128]{2,1,0:T(8,128)S(1)}, u32[]{:S(2)}, u32[]{:S(2)}) async-start(f32[16,72,128]{2,1,0:T(8,128)} %get-tuple-element.18), calls=%async_computation | async-start | bytes 1179648 | tf_op jit(solution)/shard_map/all_to_all | solution.py:235
  8.9 0.0 copy-done.1
  8.9 0.1 collective-permute-start
  9.0 1.2 %collective-permute-done = f32[8,128]{1,0:T(8,128)S(1)} collective-permute-done((f32[8,128]{1,0:T(8,128)S(1)}, f32[8,128]{1,0:T(8,128)S(1)}, u32[]{:S(2)}, u32[]{:S(2)}) %collective-permute-start) | collective-permute-done | bytes 4128 | tf_op jit(solution)/shard_map/ppermute | solution.py:234
  10.1 6.3 %collective-permute-start.1 = (f32[2,8,128]{2,1,0:T(8,128)S(1)}, f32[2,8,128]{2,1,0:T(8,128)S(1)}, u32[]{:S(2)}, u32[]{:S(2)}) collective-permute-start(f32[2,8,128]{2,1,0:T(8,128)S(1)} %pad_maximum_fusion.refs_0_), channel_id=1, source_target_pairs={{0,8},{4,12},{8,0},{12,4},{1,9},{5,13},{9,1},{13,5},{2,10},{6,14},... | collective-permute-start | bytes 24584 | tf_op jit(solution)/shard_map/ppermute | solution.py:238
  16.4 1.5 %collective-permute-start.2 = (f32[2,8,128]{2,1,0:T(8,128)S(1)}, f32[2,8,128]{2,1,0:T(8,128)S(1)}, u32[]{:S(2)}, u32[]{:S(2)}) collective-permute-start(f32[2,8,128]{2,1,0:T(8,128)S(1)} %pad_maximum_fusion.refs_0_), channel_id=1, source_target_pairs={{0,4},{4,0},{8,12},{12,8},{1,5},{5,1},{9,13},{13,9},{2,6},{6,2},{1... | collective-permute-start | bytes 24584 | tf_op jit(solution)/shard_map/ppermute | solution.py:238
  17.9 0.0 collective-permute-start.3
  17.9 0.2 collective-permute-done.1.refs_1_
  18.1 2.9 %collective-permute-done.2.refs_2_ = f32[2,8,128]{2,1,0:T(8,128)S(1)} collective-permute-done((f32[2,8,128]{2,1,0:T(8,128)S(1)}, f32[2,8,128]{2,1,0:T(8,128)S(1)}, u32[]{:S(2)}, u32[]{:S(2)}) %collective-permute-start.2) | collective-permute-done | bytes 8224 | tf_op jit(solution)/shard_map/ppermute | solution.py:238
  21.0 2.7 %collective-permute-done.3.refs_3_ = f32[2,8,128]{2,1,0:T(8,128)S(1)} collective-permute-done((f32[2,8,128]{2,1,0:T(8,128)S(1)}, f32[2,8,128]{2,1,0:T(8,128)S(1)}, u32[]{:S(2)}, u32[]{:S(2)}) %collective-permute-start.3) | collective-permute-done | bytes 8224 | tf_op jit(solution)/shard_map/ppermute | solution.py:238
  23.7 0.0 all-to-all-done.refs_4_
  23.7 1.0 %collective-permute-start.4 = (f32[16,72,128]{2,1,0:T(8,128)S(1)}, f32[16,72,128]{2,1,0:T(8,128)S(1)}, u32[]{:S(2)}, u32[]{:S(2)}) collective-permute-start(f32[16,72,128]{2,1,0:T(8,128)S(1)} %all-to-all-done.refs_4_), channel_id=1, source_target_pairs={{0,2},{2,0},{1,3},{3,1},{4,6},{6,4},{5,7},{7,5},{8,10},{10,8},{9,1... | collective-permute-start | bytes 1769480 | tf_op jit(solution)/shard_map/ppermute | solution.py:240
  24.7 0.0 copy-done
  24.7 12.4 %near_volts.1 = (bf16[512,64]{1,0:T(8,128)(2,1)S(1)}, f32[3,512,128]{2,1,0:T(8,128)S(1)}, f32[512,128]{1,0:T(8,128)S(1)}) custom-call(f32[2,8,128]{2,1,0:T(8,128)S(1)} %pad_maximum_fusion.refs_0_, f32[2,8,128]{2,1,0:T(8,128)S(1)} %collective-permute-done.1.refs_1_, f32[2,8,128]{2,1,0:T(8,128)S(1)} %collective-permute-done.2.refs_2_, ...), custom_call_target="tpu_custom_call" | custom-call | flops 3221225472 | bytes 2097152 | tf_op jit(solution)/shard_map/near_volts/pallas_call | solution.py:181
  37.1 0.3 collective-permute-done.4.sources
  37.4 12.0 %far_volts.1 = (f32[256,128]{1,0:T(8,128)S(1)}, f32[256,128]{1,0:T(8,128)S(1)}) custom-call(f32[16,72,128]{2,1,0:T(8,128)S(1)} %collective-permute-done.4.sources, f32[128,128]{1,0:T(8,128)S(1)} %copy-done, bf16[512,64]{1,0:T(8,128)(2,1)S(1)} %get-tuple-element.26.squared, f32[3,512,128]{2,1,0:T(8,128)S(1)} %get-tuple-element.27.vectors, ...), custom_call_target="tpu_custom_call" | custom-call | flops 3221225472 | bytes 2097152 | tf_op jit(solution)/shard_map/far_volts/pallas_call | solution.py:198
  49.3 0.1 collective-permute-start.5
  49.4 1.3 %collective-permute-done.5 = f32[256,128]{1,0:T(8,128)S(1)} collective-permute-done((f32[256,128]{1,0:T(8,128)S(1)}, f32[256,128]{1,0:T(8,128)S(1)}, u32[]{:S(2)}, u32[]{:S(2)}) %collective-permute-start.5) | collective-permute-done | bytes 131104 | tf_op jit(solution)/shard_map/ppermute | solution.py:243
  50.8 3.7 %collective-permute-start.6 = (f32[64,128]{1,0:T(8,128)S(1)}, f32[64,128]{1,0:T(8,128)S(1)}, u32[]{:S(2)}, u32[]{:S(2)}) collective-permute-start(f32[64,128]{1,0:T(8,128)S(1)} %get-tuple-element.31), channel_id=1, source_target_pairs={{0,8},{4,12},{8,0},{12,4},{1,9},{5,13},{9,1},{13,5},{2,10},{6,14},... | collective-permute-start | bytes 98312 | tf_op jit(solution)/shard_map/ppermute | solution.py:246
  54.5 1.5 %collective-permute-start.7 = (f32[64,128]{1,0:T(8,128)S(1)}, f32[64,128]{1,0:T(8,128)S(1)}, u32[]{:S(2)}, u32[]{:S(2)}) collective-permute-start(f32[64,128]{1,0:T(8,128)S(1)} %get-tuple-element.33), channel_id=1, source_target_pairs={{0,4},{4,0},{8,12},{12,8},{1,5},{5,1},{9,13},{13,9},{2,6},{6,2},{1... | collective-permute-start | bytes 98312 | tf_op jit(solution)/shard_map/ppermute | solution.py:246
  56.0 1.4 %collective-permute-start.8 = (f32[64,128]{1,0:T(8,128)S(1)}, f32[64,128]{1,0:T(8,128)S(1)}, u32[]{:S(2)}, u32[]{:S(2)}) collective-permute-start(f32[64,128]{1,0:T(8,128)S(1)} %get-tuple-element.32), channel_id=1, source_target_pairs={{0,12},{4,8},{8,4},{12,0},{1,13},{5,9},{9,5},{13,1},{2,14},{6,10},... | collective-permute-start | bytes 98312 | tf_op jit(solution)/shard_map/ppermute | solution.py:246
  57.4 1.4 %collective-permute-done.6 = f32[64,128]{1,0:T(8,128)S(1)} collective-permute-done((f32[64,128]{1,0:T(8,128)S(1)}, f32[64,128]{1,0:T(8,128)S(1)}, u32[]{:S(2)}, u32[]{:S(2)}) %collective-permute-start.6) | collective-permute-done | bytes 32800 | tf_op jit(solution)/shard_map/ppermute | solution.py:246
  58.8 0.6 collective-permute-done.7
  59.4 2.7 %collective-permute-done.8 = f32[64,128]{1,0:T(8,128)S(1)} collective-permute-done((f32[64,128]{1,0:T(8,128)S(1)}, f32[64,128]{1,0:T(8,128)S(1)}, u32[]{:S(2)}, u32[]{:S(2)}) %collective-permute-start.8) | collective-permute-done | bytes 32800 | tf_op jit(solution)/shard_map/ppermute | solution.py:246
  62.0 0.6 fusion.1
  (3 shorter events, 0.0 us)
Async XLA Ops:
  1.7 7.2 %copy-start.1 = (f32[8,128]{1,0:T(8,128)S(1)}, f32[8,128]{1,0:T(8,128)}, u32[]{:S(2)}) copy-start(f32[8,128]{1,0:T(8,128)} %get-tuple-element.19) | copy-start | bytes 12292
  1.7 23.0 %copy-start = (f32[128,128]{1,0:T(8,128)S(1)}, f32[128,128]{1,0:T(8,128)}, u32[]{:S(2)}) copy-start(f32[128,128]{1,0:T(8,128)} %get-tuple-element.21.refs_5_.ports) | copy-start | bytes 196612
  1.7 22.0 %all-to-all-start = ((f32[16,72,128]{2,1,0:T(8,128)}), f32[16,72,128]{2,1,0:T(8,128)S(1)}, u32[]{:S(2)}, u32[]{:S(2)}) async-start(f32[16,72,128]{2,1,0:T(8,128)} %get-tuple-element.18), calls=%async_computation | async-start | bytes 1179648 | tf_op jit(solution)/shard_map/all_to_all | solution.py:235
  8.9 1.3 %collective-permute-start = (f32[8,128]{1,0:T(8,128)S(1)}, f32[8,128]{1,0:T(8,128)S(1)}, u32[]{:S(2)}, u32[]{:S(2)}) collective-permute-start(f32[8,128]{1,0:T(8,128)S(1)} %copy-done.1), channel_id=1, source_target_pairs={{0,1},{1,0},{2,3},{3,2},{4,5},{5,4},{6,7},{7,6},{8,9},{9,8},{10,11... | collective-permute-start | bytes 12296 | tf_op jit(solution)/shard_map/ppermute | solution.py:234
  10.1 7.9 %collective-permute-start.1 = (f32[2,8,128]{2,1,0:T(8,128)S(1)}, f32[2,8,128]{2,1,0:T(8,128)S(1)}, u32[]{:S(2)}, u32[]{:S(2)}) collective-permute-start(f32[2,8,128]{2,1,0:T(8,128)S(1)} %pad_maximum_fusion.refs_0_), channel_id=1, source_target_pairs={{0,8},{4,12},{8,0},{12,4},{1,9},{5,13},{9,1},{13,5},{2,10},{6,14},... | collective-permute-start | bytes 24584 | tf_op jit(solution)/shard_map/ppermute | solution.py:238
  16.4 4.5 %collective-permute-start.2 = (f32[2,8,128]{2,1,0:T(8,128)S(1)}, f32[2,8,128]{2,1,0:T(8,128)S(1)}, u32[]{:S(2)}, u32[]{:S(2)}) collective-permute-start(f32[2,8,128]{2,1,0:T(8,128)S(1)} %pad_maximum_fusion.refs_0_), channel_id=1, source_target_pairs={{0,4},{4,0},{8,12},{12,8},{1,5},{5,1},{9,13},{13,9},{2,6},{6,2},{1... | collective-permute-start | bytes 24584 | tf_op jit(solution)/shard_map/ppermute | solution.py:238
  17.9 5.8 %collective-permute-start.3 = (f32[2,8,128]{2,1,0:T(8,128)S(1)}, f32[2,8,128]{2,1,0:T(8,128)S(1)}, u32[]{:S(2)}, u32[]{:S(2)}) collective-permute-start(f32[2,8,128]{2,1,0:T(8,128)S(1)} %pad_maximum_fusion.refs_0_), channel_id=1, source_target_pairs={{0,12},{4,8},{8,4},{12,0},{1,13},{5,9},{9,5},{13,1},{2,14},{6,10},... | collective-permute-start | bytes 24584 | tf_op jit(solution)/shard_map/ppermute | solution.py:238
  23.7 13.7 %collective-permute-start.4 = (f32[16,72,128]{2,1,0:T(8,128)S(1)}, f32[16,72,128]{2,1,0:T(8,128)S(1)}, u32[]{:S(2)}, u32[]{:S(2)}) collective-permute-start(f32[16,72,128]{2,1,0:T(8,128)S(1)} %all-to-all-done.refs_4_), channel_id=1, source_target_pairs={{0,2},{2,0},{1,3},{3,1},{4,6},{6,4},{5,7},{7,5},{8,10},{10,8},{9,1... | collective-permute-start | bytes 1769480 | tf_op jit(solution)/shard_map/ppermute | solution.py:240
  49.3 1.4 %collective-permute-start.5 = (f32[256,128]{1,0:T(8,128)S(1)}, f32[256,128]{1,0:T(8,128)S(1)}, u32[]{:S(2)}, u32[]{:S(2)}) collective-permute-start(f32[256,128]{1,0:T(8,128)S(1)} %get-tuple-element.30), channel_id=1, source_target_pairs={{0,1},{1,0},{2,3},{3,2},{4,5},{5,4},{6,7},{7,6},{8,9},{9,8},{10,11... | collective-permute-start | bytes 393224 | tf_op jit(solution)/shard_map/ppermute | solution.py:243
  50.8 8.0 %collective-permute-start.6 = (f32[64,128]{1,0:T(8,128)S(1)}, f32[64,128]{1,0:T(8,128)S(1)}, u32[]{:S(2)}, u32[]{:S(2)}) collective-permute-start(f32[64,128]{1,0:T(8,128)S(1)} %get-tuple-element.31), channel_id=1, source_target_pairs={{0,8},{4,12},{8,0},{12,4},{1,9},{5,13},{9,1},{13,5},{2,10},{6,14},... | collective-permute-start | bytes 98312 | tf_op jit(solution)/shard_map/ppermute | solution.py:246
  54.5 4.8 %collective-permute-start.7 = (f32[64,128]{1,0:T(8,128)S(1)}, f32[64,128]{1,0:T(8,128)S(1)}, u32[]{:S(2)}, u32[]{:S(2)}) collective-permute-start(f32[64,128]{1,0:T(8,128)S(1)} %get-tuple-element.33), channel_id=1, source_target_pairs={{0,4},{4,0},{8,12},{12,8},{1,5},{5,1},{9,13},{13,9},{2,6},{6,2},{1... | collective-permute-start | bytes 98312 | tf_op jit(solution)/shard_map/ppermute | solution.py:246
  56.0 6.0 %collective-permute-start.8 = (f32[64,128]{1,0:T(8,128)S(1)}, f32[64,128]{1,0:T(8,128)S(1)}, u32[]{:S(2)}, u32[]{:S(2)}) collective-permute-start(f32[64,128]{1,0:T(8,128)S(1)} %get-tuple-element.32), channel_id=1, source_target_pairs={{0,12},{4,8},{8,4},{12,0},{1,13},{5,9},{9,5},{13,1},{2,14},{6,10},... | collective-permute-start | bytes 98312 | tf_op jit(solution)/shard_map/ppermute | solution.py:246

commit v2 on v1

--- a/solution.py
+++ b/solution.py
@@ -7,8 +7,11 @@
 
 BF16 = jnp.bfloat16
 F32 = jnp.float32
-DEPTH = 64
+TILE = 256
+UNROLL = 8
+DEPTH = 32
 LANES = 128
+MIDDLE = 2.0
 COUNT = 64
 WIDTH = 1024
 AXES = ("y", "x", "zh", "zl", "c")
@@ -24,49 +27,49 @@
     return high, middle, low
 
 
-def centred(x):
+def doubled(x):
     row = lax.broadcasted_iota(jnp.int32, x.shape, 0)
-    x = jnp.where(row < 3, x - 2.0, x)
-    norm = jnp.sum(jnp.where(row < 4, x * x, 0.0), axis=0, keepdims=True)
-    return row, x, split3(norm)
+    x = jnp.concatenate([x[:4], x[:4]], 0)
+    norm = jnp.sum((x * x)[:4], axis=0, keepdims=True)
+    return row, split3(x), split3(norm)
+
+
+def by_half(row, low, high):
+    return jnp.where(row < 4, low, high)
+
+
+def by_row(row, values, rest):
+    for i, value in reversed(list(enumerate(values))):
+        rest = jnp.where(row == i, value, rest)
+    return rest
 
 
 def source_features(x):
-    row, x, (n_high, n_middle, n_low) = centred(x)
-    high, middle, low = split3(x)
-    norms = jnp.where(
-        row == 0,
-        n_high,
-        jnp.where(row == 1, n_middle, jnp.where(row == 2, n_low, jnp.where(row < 6, 1.0, 0.0))),
-    )
-    parts = [high, high, high, middle, middle, low, norms, jnp.zeros_like(x)]
-    return jnp.concatenate(parts, 0)
+    row, (high, middle, low), norm = doubled(x)
+    ones = jnp.where(row < 6, 1.0, 0.0)
+    groups = [high, by_half(row, high, middle), by_half(row, middle, low), by_row(row, norm, ones)]
+    return jnp.concatenate(groups, 0)
 
 
 def target_features(x):
-    row, x, (n_high, n_middle, n_low) = centred(x)
-    high, middle, low = split3(x)
-    norms = jnp.where(
-        row < 3,
-        1.0,
-        jnp.where(row == 3, n_high, jnp.where(row == 4, n_middle, jnp.where(row == 5, n_low, 0.0))),
-    )
-    weight = jnp.where(row < 3, -2.0, jnp.where(row == 3, 2.0, 0.0))
-    parts = [p * weight for p in (high, middle, low, high, middle, high)]
-    return jnp.concatenate(parts + [norms, jnp.zeros_like(x)], 0)
+    row, (high, middle, low), norm = doubled(x)
+    weight = jnp.where((row & 3) < 3, -2.0, 2.0)
+    groups = [by_half(row, high, middle), by_half(row, low, high), by_half(row, middle, high)]
+    last = by_row(row, (1.0, 1.0, 1.0) + norm, 0.0)
+    return jnp.concatenate([g * weight for g in groups] + [last], 0)
 
 
 def pack_kernel(t_position, t_vector, t_radius, *refs):
     position, vector, radius, current, incidence, excitation, block, copies, ports = refs
     count = t_radius.shape[1]
-    rows = [t_position[...], t_radius[...], t_vector[...], jnp.zeros((1, count), F32)]
+    rows = [t_position[...] - MIDDLE, t_radius[...], t_vector[...], jnp.zeros((1, count), F32)]
     wide = [jnp.concatenate(rows, 0), jnp.zeros((8, LANES - count), F32)]
     block[...] = jnp.concatenate(wide, 1)
     sources = copies.at[0]
     for r in range(8):
         here = slice(r * LANES, (r + 1) * LANES)
         for q in range(3):
-            sources[8 * q + r : 8 * q + r + 1, :] = position[q : q + 1, here]
+            sources[8 * q + r : 8 * q + r + 1, :] = position[q : q + 1, here] - MIDDLE
             sources[8 * q + r + 32 : 8 * q + r + 33, :] = vector[q : q + 1, here]
     sources[24:32, :] = radius[...]
     sources[56:64, :] = current[...]
@@ -101,45 +104,43 @@
     port = ports[...]
     blocks = sources.shape[0]
 
-    def prepare(b, features, raw, currents):
+    def prepare(b, features, currents):
         for r in range(WIDTH // LANES):
             here = slice(r * LANES, (r + 1) * LANES)
             x = sources[b, pl.ds(r, 8, stride=8), :]
             features[:, here] = source_features(x).astype(BF16)
-            raw[:, here] = x
             current = sources[b, pl.ds(56 + r, 1), :]
             incidence = sources[b, pl.ds(64 + r, 1), :]
             matched = jnp.where(port == incidence, current, 0.0)
             currents[here, :] = jnp.transpose(matched).astype(BF16)
 
-    def add(features, raw, currents):
-        step = 256
-        for s in range(0, WIDTH, step):
-            these = slice(s, s + step)
-            distance = jnp.dot(squared[...], features[:, these], preferred_element_type=F32)
-            alignment = []
-            for t in range(s, s + step, LANES):
-                here = slice(t, t + LANES)
-                alignment.append(
-                    vectors[0] * raw[4:5, here]
-                    + vectors[1] * raw[5:6, here]
-                    + vectors[2] * raw[6:7, here]
-                )
-            inductance = jnp.concatenate(alignment, 1) * lax.rsqrt(distance)
+    def inductance(b, k, features):
+        these = slice(k * TILE, (k + 1) * TILE)
+        distance = jnp.dot(squared[...], features[:, these], preferred_element_type=F32)
+        alignment = []
+        for r in range(k * TILE // LANES, (k + 1) * TILE // LANES):
+            x, y, z = (sources[b, pl.ds(8 * d + r, 1), :] for d in (4, 5, 6))
+            alignment.append(vectors[0] * x + vectors[1] * y + vectors[2] * z)
+        return (jnp.concatenate(alignment, 1) * lax.rsqrt(distance)).astype(BF16)
+
+    def add(b, features, currents):
+        for k in range(WIDTH // TILE):
+            these = slice(k * TILE, (k + 1) * TILE)
             total[...] += jnp.dot(
-                inductance.astype(BF16), currents[these, :], preferred_element_type=F32
+                inductance(b, k, features), currents[these, :], preferred_element_type=F32
             )
 
     prepare(0, *even)
 
-    def two(i, carry):
-        prepare(2 * i + 1, *odd)
-        add(*even)
-        prepare(jnp.minimum(2 * i + 2, blocks - 1), *even)
-        add(*odd)
+    def some(i, carry):
+        for j in range(UNROLL):
+            b = UNROLL * i + j
+            this, other = (even, odd) if j % 2 == 0 else (odd, even)
+            prepare(jnp.minimum(b + 1, blocks - 1), *other)
+            add(b, *this)
         return carry
 
-    lax.fori_loop(0, blocks // 2, two, 0)
+    lax.fori_loop(0, blocks // UNROLL, some, 0)
 
 
 def near_kernel(*refs):
@@ -147,23 +148,19 @@
     sources, ports, squared, vectors, total, *buffers = refs
     prepare_targets(pairs, squared, vectors)
     total[...] = jnp.zeros_like(total)
-    add_sources(sources, ports, squared, vectors, total, buffers[:3], buffers[3:])
+    add_sources(sources, ports, squared, vectors, total, buffers[:2], buffers[2:])
 
 
 def far_kernel(sources, ports, squared, vectors, start, keep, send, total, *buffers):
     total[...] = start[...]
-    add_sources(sources, ports, squared, vectors, total, buffers[:3], buffers[3:])
+    add_sources(sources, ports, squared, vectors, total, buffers[:2], buffers[2:])
     half = total.shape[0] // 2
     keep[...] = total[:half, :]
     send[...] = total[half:, :]
 
 
 ROWS = 2 * len(FLIPS) * COUNT
-BUFFERS = [
-    pltpu.VMEM((DEPTH, WIDTH), BF16),
-    pltpu.VMEM((8, WIDTH), F32),
-    pltpu.VMEM((WIDTH, LANES), BF16),
-] * 2
+BUFFERS = [pltpu.VMEM((DEPTH, WIDTH), BF16), pltpu.VMEM((WIDTH, LANES), BF16)] * 2
 
 
 def options(sources):

time: 63.3 us -> 62.9 us (level)
  Pallas kernels: 26.1 us -> 25.2 us
  transfers between devices with their start and end apart: 10 -> 10, of which waited for: 9 -> 9; matrix products, arithmetic and copies ran while one was open for 0% -> 0% of each run, Pallas kernels for 20% -> 19%
where the time goes in v2:
time: 62.9 us; the launch traced here: 62.2 us
  Pallas kernels  25.2 us (40%)
  starting transfers between devices  22.7 us (36%)
  waiting for transfers between devices  13.6 us (22%)
  other arithmetic  0.64 us (1%)
    pallas_call x1, Pallas kernels, near_volts(): pl.pallas_call(near_kernel, out_shape=[jax.ShapeDtypeStruct((ROWS, DEPTH)...  11.9 us
    pallas_call x1, Pallas kernels, far_volts(): pl.pallas_call(far_kernel, out_shape=[jax.ShapeDtypeStruct((ROWS // 2, LA...  11.5 us
    ppermute x3, starting transfers between devices, per_device(): lax.ppermute(pair, 'zh', [(i, i ^ k) for i in zh])  7.77 us
    all_to_all x1, starting transfers between devices, per_device(): sources = lax.all_to_all(copies, ('y', 'x'), 0, 0, tiled=True)  7.17 us
    ppermute x3, starting transfers between devices, per_device(): shares.append(lax.ppermute(partial[j], 'zh', [(i, i ^ k) for i in zh]))  6.58 us
    ppermute x3, waiting for transfers between devices, per_device(): lax.ppermute(pair, 'zh', [(i, i ^ k) for i in zh])  5.76 us
    ppermute x3, waiting for transfers between devices, per_device(): shares.append(lax.ppermute(partial[j], 'zh', [(i, i ^ k) for i in zh]))  4.66 us
    pallas_call x1, Pallas kernels, pack(): pl.pallas_call(pack_kernel, out_shape=[jax.ShapeDtypeStruct(shape, F32) f...  1.7 us
  transfers between devices with their start and end apart: 10, of which 9 were waited for; matrix products, arithmetic and copies ran while one was open for 0% of the time, Pallas kernels for 19%

profile of v2, /device:TPU:32, one launch (start us, length us, event | category | flops | bytes accessed | tf_op | source)
XLA Modules:
  0.0 62.2 jit_solution(13940125654036942651)
XLA Ops:
  0.0 1.7 %pack.1 = (f32[8,128]{1,0:T(8,128)}, f32[16,72,128]{2,1,0:T(8,128)}, f32[128,128]{1,0:T(8,128)}) custom-call(f32[3,64]{1,0:T(4,128)} %t_position.1, f32[3,64]{1,0:T(4,128)} %t_vector.1, f32[1,64]{1,0:T(1,128)} %bitcast.12, f32[3,1024]{1,0:T(4,128)} %refs_0_.1, f32[3,1024]{1,0:T(4,128)} %refs_1_.1, f32[8,128]{1,0:T(8,128)} %bitcast.7, f32[8,128]{1,0:T(8,128)} %bitcast.8, ...), custom_call_target="tpu_custom_call" | custom-call | tf_op jit(solution)/shard_map/pack/pallas_call | solution.py:84
  1.7 0.0 copy-start.1
  1.7 0.0 copy-start
  1.7 7.2 %all-to-all-start = ((f32[16,72,128]{2,1,0:T(8,128)}), f32[16,72,128]{2,1,0:T(8,128)S(1)}, u32[]{:S(2)}, u32[]{:S(2)}) async-start(f32[16,72,128]{2,1,0:T(8,128)} %get-tuple-element.18), calls=%async_computation | async-start | bytes 1179648 | tf_op jit(solution)/shard_map/all_to_all | solution.py:232
  8.9 0.0 copy-done.1
  8.9 0.1 collective-permute-start
  9.0 1.2 %collective-permute-done = f32[8,128]{1,0:T(8,128)S(1)} collective-permute-done((f32[8,128]{1,0:T(8,128)S(1)}, f32[8,128]{1,0:T(8,128)S(1)}, u32[]{:S(2)}, u32[]{:S(2)}) %collective-permute-start) | collective-permute-done | bytes 4128 | tf_op jit(solution)/shard_map/ppermute | solution.py:231
  10.1 6.3 %collective-permute-start.1 = (f32[2,8,128]{2,1,0:T(8,128)S(1)}, f32[2,8,128]{2,1,0:T(8,128)S(1)}, u32[]{:S(2)}, u32[]{:S(2)}) collective-permute-start(f32[2,8,128]{2,1,0:T(8,128)S(1)} %pad_maximum_fusion.refs_0_), channel_id=1, source_target_pairs={{0,8},{4,12},{8,0},{12,4},{1,9},{5,13},{9,1},{13,5},{2,10},{6,14},... | collective-permute-start | bytes 24584 | tf_op jit(solution)/shard_map/ppermute | solution.py:235
  16.4 1.5 %collective-permute-start.2 = (f32[2,8,128]{2,1,0:T(8,128)S(1)}, f32[2,8,128]{2,1,0:T(8,128)S(1)}, u32[]{:S(2)}, u32[]{:S(2)}) collective-permute-start(f32[2,8,128]{2,1,0:T(8,128)S(1)} %pad_maximum_fusion.refs_0_), channel_id=1, source_target_pairs={{0,4},{4,0},{8,12},{12,8},{1,5},{5,1},{9,13},{13,9},{2,6},{6,2},{1... | collective-permute-start | bytes 24584 | tf_op jit(solution)/shard_map/ppermute | solution.py:235
  17.9 0.0 collective-permute-start.3
  17.9 0.2 collective-permute-done.1.refs_1_
  18.1 2.9 %collective-permute-done.2.refs_2_ = f32[2,8,128]{2,1,0:T(8,128)S(1)} collective-permute-done((f32[2,8,128]{2,1,0:T(8,128)S(1)}, f32[2,8,128]{2,1,0:T(8,128)S(1)}, u32[]{:S(2)}, u32[]{:S(2)}) %collective-permute-start.2) | collective-permute-done | bytes 8224 | tf_op jit(solution)/shard_map/ppermute | solution.py:235
  21.0 2.7 %collective-permute-done.3.refs_3_ = f32[2,8,128]{2,1,0:T(8,128)S(1)} collective-permute-done((f32[2,8,128]{2,1,0:T(8,128)S(1)}, f32[2,8,128]{2,1,0:T(8,128)S(1)}, u32[]{:S(2)}, u32[]{:S(2)}) %collective-permute-start.3) | collective-permute-done | bytes 8224 | tf_op jit(solution)/shard_map/ppermute | solution.py:235
  23.7 0.0 all-to-all-done.refs_4_
  23.7 1.0 %collective-permute-start.4 = (f32[16,72,128]{2,1,0:T(8,128)S(1)}, f32[16,72,128]{2,1,0:T(8,128)S(1)}, u32[]{:S(2)}, u32[]{:S(2)}) collective-permute-start(f32[16,72,128]{2,1,0:T(8,128)S(1)} %all-to-all-done.refs_4_), channel_id=1, source_target_pairs={{0,2},{2,0},{1,3},{3,1},{4,6},{6,4},{5,7},{7,5},{8,10},{10,8},{9,1... | collective-permute-start | bytes 1769480 | tf_op jit(solution)/shard_map/ppermute | solution.py:237
  24.7 0.0 copy-done
  24.7 11.9 %near_volts.1 = (bf16[512,32]{1,0:T(8,128)(2,1)S(1)}, f32[3,512,128]{2,1,0:T(8,128)S(1)}, f32[512,128]{1,0:T(8,128)S(1)}) custom-call(f32[2,8,128]{2,1,0:T(8,128)S(1)} %pad_maximum_fusion.refs_0_, f32[2,8,128]{2,1,0:T(8,128)S(1)} %collective-permute-done.1.refs_1_, f32[2,8,128]{2,1,0:T(8,128)S(1)} %collective-permute-done.2.refs_2_, ...), custom_call_target="tpu_custom_call" | custom-call | flops 2684354560 | bytes 2097152 | tf_op jit(solution)/shard_map/near_volts/pallas_call | solution.py:178
  36.6 0.7 %collective-permute-done.4.sources = f32[16,72,128]{2,1,0:T(8,128)S(1)} collective-permute-done((f32[16,72,128]{2,1,0:T(8,128)S(1)}, f32[16,72,128]{2,1,0:T(8,128)S(1)}, u32[]{:S(2)}, u32[]{:S(2)}) %collective-permute-start.4) | collective-permute-done | bytes 589856 | tf_op jit(solution)/shard_map/ppermute | solution.py:237
  37.4 11.5 %far_volts.1 = (f32[256,128]{1,0:T(8,128)S(1)}, f32[256,128]{1,0:T(8,128)S(1)}) custom-call(f32[16,72,128]{2,1,0:T(8,128)S(1)} %collective-permute-done.4.sources, f32[128,128]{1,0:T(8,128)S(1)} %copy-done, bf16[512,32]{1,0:T(8,128)(2,1)S(1)} %get-tuple-element.26.squared, f32[3,512,128]{2,1,0:T(8,128)S(1)} %get-tuple-element.27.vectors, ...), custom_call_target="tpu_custom_call" | custom-call | flops 2684354560 | bytes 2097152 | tf_op jit(solution)/shard_map/far_volts/pallas_call | solution.py:195
  48.9 0.1 collective-permute-start.5
  49.0 1.3 %collective-permute-done.5 = f32[256,128]{1,0:T(8,128)S(1)} collective-permute-done((f32[256,128]{1,0:T(8,128)S(1)}, f32[256,128]{1,0:T(8,128)S(1)}, u32[]{:S(2)}, u32[]{:S(2)}) %collective-permute-start.5) | collective-permute-done | bytes 131104 | tf_op jit(solution)/shard_map/ppermute | solution.py:240
  50.4 3.7 %collective-permute-start.6 = (f32[64,128]{1,0:T(8,128)S(1)}, f32[64,128]{1,0:T(8,128)S(1)}, u32[]{:S(2)}, u32[]{:S(2)}) collective-permute-start(f32[64,128]{1,0:T(8,128)S(1)} %get-tuple-element.31), channel_id=1, source_target_pairs={{0,8},{4,12},{8,0},{12,4},{1,9},{5,13},{9,1},{13,5},{2,10},{6,14},... | collective-permute-start | bytes 98312 | tf_op jit(solution)/shard_map/ppermute | solution.py:243
  54.1 1.5 %collective-permute-start.7 = (f32[64,128]{1,0:T(8,128)S(1)}, f32[64,128]{1,0:T(8,128)S(1)}, u32[]{:S(2)}, u32[]{:S(2)}) collective-permute-start(f32[64,128]{1,0:T(8,128)S(1)} %get-tuple-element.33), channel_id=1, source_target_pairs={{0,4},{4,0},{8,12},{12,8},{1,5},{5,1},{9,13},{13,9},{2,6},{6,2},{1... | collective-permute-start | bytes 98312 | tf_op jit(solution)/shard_map/ppermute | solution.py:243
  55.6 1.4 %collective-permute-start.8 = (f32[64,128]{1,0:T(8,128)S(1)}, f32[64,128]{1,0:T(8,128)S(1)}, u32[]{:S(2)}, u32[]{:S(2)}) collective-permute-start(f32[64,128]{1,0:T(8,128)S(1)} %get-tuple-element.32), channel_id=1, source_target_pairs={{0,12},{4,8},{8,4},{12,0},{1,13},{5,9},{9,5},{13,1},{2,14},{6,10},... | collective-permute-start | bytes 98312 | tf_op jit(solution)/shard_map/ppermute | solution.py:243
  57.0 1.4 %collective-permute-done.6 = f32[64,128]{1,0:T(8,128)S(1)} collective-permute-done((f32[64,128]{1,0:T(8,128)S(1)}, f32[64,128]{1,0:T(8,128)S(1)}, u32[]{:S(2)}, u32[]{:S(2)}) %collective-permute-start.6) | collective-permute-done | bytes 32800 | tf_op jit(solution)/shard_map/ppermute | solution.py:243
  58.4 0.6 collective-permute-done.7
  59.0 2.7 %collective-permute-done.8 = f32[64,128]{1,0:T(8,128)S(1)} collective-permute-done((f32[64,128]{1,0:T(8,128)S(1)}, f32[64,128]{1,0:T(8,128)S(1)}, u32[]{:S(2)}, u32[]{:S(2)}) %collective-permute-start.8) | collective-permute-done | bytes 32800 | tf_op jit(solution)/shard_map/ppermute | solution.py:243
  61.6 0.6 %fusion.1 = f32[64,128]{1,0:T(8,128)} fusion(f32[64,128]{1,0:T(8,128)S(1)} %collective-permute-done.8, f32[64,128]{1,0:T(8,128)S(1)} %collective-permute-done.7, f32[64,128]{1,0:T(8,128)S(1)} %collective-permute-done.6, f32[256,128]{1,0:T(8,128)S(1)} %add.12), kind=kLoop, calls=%fused_computation.2 | loop fusion | flops 24576 | bytes 163840 | tf_op jit(solution)/shard_map/add | solution.py:244
  (3 shorter events, 0.0 us)
Async XLA Ops:
  1.7 7.2 %copy-start.1 = (f32[8,128]{1,0:T(8,128)S(1)}, f32[8,128]{1,0:T(8,128)}, u32[]{:S(2)}) copy-start(f32[8,128]{1,0:T(8,128)} %get-tuple-element.19) | copy-start | bytes 12292
  1.7 23.0 %copy-start = (f32[128,128]{1,0:T(8,128)S(1)}, f32[128,128]{1,0:T(8,128)}, u32[]{:S(2)}) copy-start(f32[128,128]{1,0:T(8,128)} %get-tuple-element.21.refs_5_.ports) | copy-start | bytes 196612
  1.7 22.0 %all-to-all-start = ((f32[16,72,128]{2,1,0:T(8,128)}), f32[16,72,128]{2,1,0:T(8,128)S(1)}, u32[]{:S(2)}, u32[]{:S(2)}) async-start(f32[16,72,128]{2,1,0:T(8,128)} %get-tuple-element.18), calls=%async_computation | async-start | bytes 1179648 | tf_op jit(solution)/shard_map/all_to_all | solution.py:232
  8.9 1.3 %collective-permute-start = (f32[8,128]{1,0:T(8,128)S(1)}, f32[8,128]{1,0:T(8,128)S(1)}, u32[]{:S(2)}, u32[]{:S(2)}) collective-permute-start(f32[8,128]{1,0:T(8,128)S(1)} %copy-done.1), channel_id=1, source_target_pairs={{0,1},{1,0},{2,3},{3,2},{4,5},{5,4},{6,7},{7,6},{8,9},{9,8},{10,11... | collective-permute-start | bytes 12296 | tf_op jit(solution)/shard_map/ppermute | solution.py:231
  10.1 7.9 %collective-permute-start.1 = (f32[2,8,128]{2,1,0:T(8,128)S(1)}, f32[2,8,128]{2,1,0:T(8,128)S(1)}, u32[]{:S(2)}, u32[]{:S(2)}) collective-permute-start(f32[2,8,128]{2,1,0:T(8,128)S(1)} %pad_maximum_fusion.refs_0_), channel_id=1, source_target_pairs={{0,8},{4,12},{8,0},{12,4},{1,9},{5,13},{9,1},{13,5},{2,10},{6,14},... | collective-permute-start | bytes 24584 | tf_op jit(solution)/shard_map/ppermute | solution.py:235
  16.4 4.5 %collective-permute-start.2 = (f32[2,8,128]{2,1,0:T(8,128)S(1)}, f32[2,8,128]{2,1,0:T(8,128)S(1)}, u32[]{:S(2)}, u32[]{:S(2)}) collective-permute-start(f32[2,8,128]{2,1,0:T(8,128)S(1)} %pad_maximum_fusion.refs_0_), channel_id=1, source_target_pairs={{0,4},{4,0},{8,12},{12,8},{1,5},{5,1},{9,13},{13,9},{2,6},{6,2},{1... | collective-permute-start | bytes 24584 | tf_op jit(solution)/shard_map/ppermute | solution.py:235
  17.9 5.8 %collective-permute-start.3 = (f32[2,8,128]{2,1,0:T(8,128)S(1)}, f32[2,8,128]{2,1,0:T(8,128)S(1)}, u32[]{:S(2)}, u32[]{:S(2)}) collective-permute-start(f32[2,8,128]{2,1,0:T(8,128)S(1)} %pad_maximum_fusion.refs_0_), channel_id=1, source_target_pairs={{0,12},{4,8},{8,4},{12,0},{1,13},{5,9},{9,5},{13,1},{2,14},{6,10},... | collective-permute-start | bytes 24584 | tf_op jit(solution)/shard_map/ppermute | solution.py:235
  23.7 13.7 %collective-permute-start.4 = (f32[16,72,128]{2,1,0:T(8,128)S(1)}, f32[16,72,128]{2,1,0:T(8,128)S(1)}, u32[]{:S(2)}, u32[]{:S(2)}) collective-permute-start(f32[16,72,128]{2,1,0:T(8,128)S(1)} %all-to-all-done.refs_4_), channel_id=1, source_target_pairs={{0,2},{2,0},{1,3},{3,1},{4,6},{6,4},{5,7},{7,5},{8,10},{10,8},{9,1... | collective-permute-start | bytes 1769480 | tf_op jit(solution)/shard_map/ppermute | solution.py:237
  48.9 1.4 %collective-permute-start.5 = (f32[256,128]{1,0:T(8,128)S(1)}, f32[256,128]{1,0:T(8,128)S(1)}, u32[]{:S(2)}, u32[]{:S(2)}) collective-permute-start(f32[256,128]{1,0:T(8,128)S(1)} %get-tuple-element.30), channel_id=1, source_target_pairs={{0,1},{1,0},{2,3},{3,2},{4,5},{5,4},{6,7},{7,6},{8,9},{9,8},{10,11... | collective-permute-start | bytes 393224 | tf_op jit(solution)/shard_map/ppermute | solution.py:240
  50.4 8.0 %collective-permute-start.6 = (f32[64,128]{1,0:T(8,128)S(1)}, f32[64,128]{1,0:T(8,128)S(1)}, u32[]{:S(2)}, u32[]{:S(2)}) collective-permute-start(f32[64,128]{1,0:T(8,128)S(1)} %get-tuple-element.31), channel_id=1, source_target_pairs={{0,8},{4,12},{8,0},{12,4},{1,9},{5,13},{9,1},{13,5},{2,10},{6,14},... | collective-permute-start | bytes 98312 | tf_op jit(solution)/shard_map/ppermute | solution.py:243
  54.1 4.8 %collective-permute-start.7 = (f32[64,128]{1,0:T(8,128)S(1)}, f32[64,128]{1,0:T(8,128)S(1)}, u32[]{:S(2)}, u32[]{:S(2)}) collective-permute-start(f32[64,128]{1,0:T(8,128)S(1)} %get-tuple-element.33), channel_id=1, source_target_pairs={{0,4},{4,0},{8,12},{12,8},{1,5},{5,1},{9,13},{13,9},{2,6},{6,2},{1... | collective-permute-start | bytes 98312 | tf_op jit(solution)/shard_map/ppermute | solution.py:243
  55.6 6.0 %collective-permute-start.8 = (f32[64,128]{1,0:T(8,128)S(1)}, f32[64,128]{1,0:T(8,128)S(1)}, u32[]{:S(2)}, u32[]{:S(2)}) collective-permute-start(f32[64,128]{1,0:T(8,128)S(1)} %get-tuple-element.32), channel_id=1, source_target_pairs={{0,12},{4,8},{8,4},{12,0},{1,13},{5,9},{9,5},{13,1},{2,14},{6,10},... | collective-permute-start | bytes 98312 | tf_op jit(solution)/shard_map/ppermute | solution.py:243

commit v3 on v2

--- a/solution.py
+++ b/solution.py
@@ -8,7 +8,7 @@
 BF16 = jnp.bfloat16
 F32 = jnp.float32
 TILE = 256
-UNROLL = 8
+UNROLL = 16
 DEPTH = 32
 LANES = 128
 MIDDLE = 2.0
@@ -91,13 +91,14 @@
 
 
 def prepare_targets(pairs, squared, vectors):
-    for j in range(2 * len(FLIPS)):
-        here = slice(j * COUNT, (j + 1) * COUNT)
-        x = pairs[j % len(FLIPS)][j // len(FLIPS)]
-        squared[here, :] = jnp.transpose(target_features(x))[:COUNT].astype(BF16)
+    for j in range(len(FLIPS)):
+        here = slice(2 * j * COUNT, 2 * (j + 1) * COUNT)
+        x = jnp.concatenate([pairs[j][0][:, :COUNT], pairs[j][1][:, :COUNT]], 1)
+        squared[here, :] = jnp.transpose(target_features(x)).astype(BF16)
         for d in range(3):
-            spread = jnp.broadcast_to(x[4 + d : 5 + d, :], (LANES, LANES))
-            vectors[d, here, :] = jnp.transpose(spread)[:COUNT]
+            vectors[d, here, :] = jnp.transpose(
+                jnp.broadcast_to(x[4 + d : 5 + d, :], (2 * COUNT, LANES))
+            )
 
 
 def add_sources(sources, ports, squared, vectors, total, even, odd):
@@ -154,9 +155,10 @@
 def far_kernel(sources, ports, squared, vectors, start, keep, send, total, *buffers):
     total[...] = start[...]
     add_sources(sources, ports, squared, vectors, total, buffers[:2], buffers[2:])
-    half = total.shape[0] // 2
-    keep[...] = total[:half, :]
-    send[...] = total[half:, :]
+    for j in range(len(FLIPS)):
+        here = slice(j * COUNT, (j + 1) * COUNT)
+        keep[here, :] = total[2 * j * COUNT : (2 * j + 1) * COUNT, :]
+        send[here, :] = total[(2 * j + 1) * COUNT : 2 * (j + 1) * COUNT, :]
 
 
 ROWS = 2 * len(FLIPS) * COUNT

time: 62.9 us -> 62.9 us (level)
  waiting for transfers between devices: 13.6 us -> 14.5 us
  Pallas kernels: 25.2 us -> 24.3 us
    ppermute x1, waiting for transfers between devices: 0.72 us -> 1.55 us  [per_device(): far = lax.ppermute(sources, 'zl', swap)]
    pallas_call x1, Pallas kernels: 11.9 us -> 11.1 us  [near_volts(): pl.pallas_call(near_kernel, out_shape=[jax.ShapeDtypeStruct((ROWS, DEPTH)...]
  transfers between devices with their start and end apart: 10 -> 10, of which waited for: 9 -> 9; matrix products, arithmetic and copies ran while one was open for 0% -> 0% of each run, Pallas kernels for 19% -> 18%
where the time goes in v3:
time: 62.9 us; the launch traced here: 62.2 us
  Pallas kernels  24.3 us (39%)
  starting transfers between devices  22.7 us (36%)
  waiting for transfers between devices  14.5 us (23%)
  other arithmetic  0.64 us (1%)
    pallas_call x1, Pallas kernels, far_volts(): pl.pallas_call(far_kernel, out_shape=[jax.ShapeDtypeStruct((ROWS // 2, LA...  11.5 us
    pallas_call x1, Pallas kernels, near_volts(): pl.pallas_call(near_kernel, out_shape=[jax.ShapeDtypeStruct((ROWS, DEPTH)...  11.1 us
    ppermute x3, starting transfers between devices, per_device(): lax.ppermute(pair, 'zh', [(i, i ^ k) for i in zh])  7.77 us
    all_to_all x1, starting transfers between devices, per_device(): sources = lax.all_to_all(copies, ('y', 'x'), 0, 0, tiled=True)  7.17 us
    ppermute x3, starting transfers between devices, per_device(): shares.append(lax.ppermute(partial[j], 'zh', [(i, i ^ k) for i in zh]))  6.58 us
    ppermute x3, waiting for transfers between devices, per_device(): lax.ppermute(pair, 'zh', [(i, i ^ k) for i in zh])  5.76 us
    ppermute x3, waiting for transfers between devices, per_device(): shares.append(lax.ppermute(partial[j], 'zh', [(i, i ^ k) for i in zh]))  4.66 us
    pallas_call x1, Pallas kernels, pack(): pl.pallas_call(pack_kernel, out_shape=[jax.ShapeDtypeStruct(shape, F32) f...  1.7 us
  transfers between devices with their start and end apart: 10, of which 9 were waited for; matrix products, arithmetic and copies ran while one was open for 0% of the time, Pallas kernels for 18%

profile of v3, /device:TPU:32, one launch (start us, length us, event | category | flops | bytes accessed | tf_op | source)
XLA Modules:
  0.0 62.2 jit_solution(7096159731099555722)
XLA Ops:
  0.0 1.7 %pack.1 = (f32[8,128]{1,0:T(8,128)}, f32[16,72,128]{2,1,0:T(8,128)}, f32[128,128]{1,0:T(8,128)}) custom-call(f32[3,64]{1,0:T(4,128)} %t_position.1, f32[3,64]{1,0:T(4,128)} %t_vector.1, f32[1,64]{1,0:T(1,128)} %bitcast.12, f32[3,1024]{1,0:T(4,128)} %refs_0_.1, f32[3,1024]{1,0:T(4,128)} %refs_1_.1, f32[8,128]{1,0:T(8,128)} %bitcast.7, f32[8,128]{1,0:T(8,128)} %bitcast.8, ...), custom_call_target="tpu_custom_call" | custom-call | tf_op jit(solution)/shard_map/pack/pallas_call | solution.py:84
  1.7 0.0 copy-start.1
  1.7 0.0 copy-start
  1.7 7.2 %all-to-all-start = ((f32[16,72,128]{2,1,0:T(8,128)}), f32[16,72,128]{2,1,0:T(8,128)S(1)}, u32[]{:S(2)}, u32[]{:S(2)}) async-start(f32[16,72,128]{2,1,0:T(8,128)} %get-tuple-element.18), calls=%async_computation | async-start | bytes 1179648 | tf_op jit(solution)/shard_map/all_to_all | solution.py:234
  8.9 0.0 copy-done.1
  8.9 0.1 collective-permute-start
  9.0 1.2 %collective-permute-done = f32[8,128]{1,0:T(8,128)S(1)} collective-permute-done((f32[8,128]{1,0:T(8,128)S(1)}, f32[8,128]{1,0:T(8,128)S(1)}, u32[]{:S(2)}, u32[]{:S(2)}) %collective-permute-start) | collective-permute-done | bytes 4128 | tf_op jit(solution)/shard_map/ppermute | solution.py:233
  10.1 6.3 %collective-permute-start.1 = (f32[2,8,128]{2,1,0:T(8,128)S(1)}, f32[2,8,128]{2,1,0:T(8,128)S(1)}, u32[]{:S(2)}, u32[]{:S(2)}) collective-permute-start(f32[2,8,128]{2,1,0:T(8,128)S(1)} %pad_maximum_fusion.refs_0_), channel_id=1, source_target_pairs={{0,8},{4,12},{8,0},{12,4},{1,9},{5,13},{9,1},{13,5},{2,10},{6,14},... | collective-permute-start | bytes 24584 | tf_op jit(solution)/shard_map/ppermute | solution.py:237
  16.4 1.5 %collective-permute-start.2 = (f32[2,8,128]{2,1,0:T(8,128)S(1)}, f32[2,8,128]{2,1,0:T(8,128)S(1)}, u32[]{:S(2)}, u32[]{:S(2)}) collective-permute-start(f32[2,8,128]{2,1,0:T(8,128)S(1)} %pad_maximum_fusion.refs_0_), channel_id=1, source_target_pairs={{0,4},{4,0},{8,12},{12,8},{1,5},{5,1},{9,13},{13,9},{2,6},{6,2},{1... | collective-permute-start | bytes 24584 | tf_op jit(solution)/shard_map/ppermute | solution.py:237
  17.9 0.0 collective-permute-start.3
  17.9 0.2 collective-permute-done.1.refs_1_
  18.1 2.9 %collective-permute-done.2.refs_2_ = f32[2,8,128]{2,1,0:T(8,128)S(1)} collective-permute-done((f32[2,8,128]{2,1,0:T(8,128)S(1)}, f32[2,8,128]{2,1,0:T(8,128)S(1)}, u32[]{:S(2)}, u32[]{:S(2)}) %collective-permute-start.2) | collective-permute-done | bytes 8224 | tf_op jit(solution)/shard_map/ppermute | solution.py:237
  21.0 2.7 %collective-permute-done.3.refs_3_ = f32[2,8,128]{2,1,0:T(8,128)S(1)} collective-permute-done((f32[2,8,128]{2,1,0:T(8,128)S(1)}, f32[2,8,128]{2,1,0:T(8,128)S(1)}, u32[]{:S(2)}, u32[]{:S(2)}) %collective-permute-start.3) | collective-permute-done | bytes 8224 | tf_op jit(solution)/shard_map/ppermute | solution.py:237
  23.7 0.0 all-to-all-done.refs_4_
  23.7 1.0 %collective-permute-start.4 = (f32[16,72,128]{2,1,0:T(8,128)S(1)}, f32[16,72,128]{2,1,0:T(8,128)S(1)}, u32[]{:S(2)}, u32[]{:S(2)}) collective-permute-start(f32[16,72,128]{2,1,0:T(8,128)S(1)} %all-to-all-done.refs_4_), channel_id=1, source_target_pairs={{0,2},{2,0},{1,3},{3,1},{4,6},{6,4},{5,7},{7,5},{8,10},{10,8},{9,1... | collective-permute-start | bytes 1769480 | tf_op jit(solution)/shard_map/ppermute | solution.py:239
  24.7 0.0 copy-done
  24.7 11.1 %near_volts.1 = (bf16[512,32]{1,0:T(8,128)(2,1)S(1)}, f32[3,512,128]{2,1,0:T(8,128)S(1)}, f32[512,128]{1,0:T(8,128)S(1)}) custom-call(f32[2,8,128]{2,1,0:T(8,128)S(1)} %pad_maximum_fusion.refs_0_, f32[2,8,128]{2,1,0:T(8,128)S(1)} %collective-permute-done.1.refs_1_, f32[2,8,128]{2,1,0:T(8,128)S(1)} %collective-permute-done.2.refs_2_, ...), custom_call_target="tpu_custom_call" | custom-call | flops 2684354560 | bytes 2097152 | tf_op jit(solution)/shard_map/near_volts/pallas_call | solution.py:180
  35.8 1.6 %collective-permute-done.4.sources = f32[16,72,128]{2,1,0:T(8,128)S(1)} collective-permute-done((f32[16,72,128]{2,1,0:T(8,128)S(1)}, f32[16,72,128]{2,1,0:T(8,128)S(1)}, u32[]{:S(2)}, u32[]{:S(2)}) %collective-permute-start.4) | collective-permute-done | bytes 589856 | tf_op jit(solution)/shard_map/ppermute | solution.py:239
  37.4 11.5 %far_volts.1 = (f32[256,128]{1,0:T(8,128)S(1)}, f32[256,128]{1,0:T(8,128)S(1)}) custom-call(f32[16,72,128]{2,1,0:T(8,128)S(1)} %collective-permute-done.4.sources, f32[128,128]{1,0:T(8,128)S(1)} %copy-done, bf16[512,32]{1,0:T(8,128)(2,1)S(1)} %get-tuple-element.26.squared, f32[3,512,128]{2,1,0:T(8,128)S(1)} %get-tuple-element.27.vectors, ...), custom_call_target="tpu_custom_call" | custom-call | flops 2684354560 | bytes 2097152 | tf_op jit(solution)/shard_map/far_volts/pallas_call | solution.py:197
  48.9 0.1 collective-permute-start.5
  49.0 1.3 %collective-permute-done.5 = f32[256,128]{1,0:T(8,128)S(1)} collective-permute-done((f32[256,128]{1,0:T(8,128)S(1)}, f32[256,128]{1,0:T(8,128)S(1)}, u32[]{:S(2)}, u32[]{:S(2)}) %collective-permute-start.5) | collective-permute-done | bytes 131104 | tf_op jit(solution)/shard_map/ppermute | solution.py:242
  50.4 3.7 %collective-permute-start.6 = (f32[64,128]{1,0:T(8,128)S(1)}, f32[64,128]{1,0:T(8,128)S(1)}, u32[]{:S(2)}, u32[]{:S(2)}) collective-permute-start(f32[64,128]{1,0:T(8,128)S(1)} %get-tuple-element.31), channel_id=1, source_target_pairs={{0,8},{4,12},{8,0},{12,4},{1,9},{5,13},{9,1},{13,5},{2,10},{6,14},... | collective-permute-start | bytes 98312 | tf_op jit(solution)/shard_map/ppermute | solution.py:245
  54.1 1.5 %collective-permute-start.7 = (f32[64,128]{1,0:T(8,128)S(1)}, f32[64,128]{1,0:T(8,128)S(1)}, u32[]{:S(2)}, u32[]{:S(2)}) collective-permute-start(f32[64,128]{1,0:T(8,128)S(1)} %get-tuple-element.33), channel_id=1, source_target_pairs={{0,4},{4,0},{8,12},{12,8},{1,5},{5,1},{9,13},{13,9},{2,6},{6,2},{1... | collective-permute-start | bytes 98312 | tf_op jit(solution)/shard_map/ppermute | solution.py:245
  55.6 1.4 %collective-permute-start.8 = (f32[64,128]{1,0:T(8,128)S(1)}, f32[64,128]{1,0:T(8,128)S(1)}, u32[]{:S(2)}, u32[]{:S(2)}) collective-permute-start(f32[64,128]{1,0:T(8,128)S(1)} %get-tuple-element.32), channel_id=1, source_target_pairs={{0,12},{4,8},{8,4},{12,0},{1,13},{5,9},{9,5},{13,1},{2,14},{6,10},... | collective-permute-start | bytes 98312 | tf_op jit(solution)/shard_map/ppermute | solution.py:245
  56.9 1.4 %collective-permute-done.6 = f32[64,128]{1,0:T(8,128)S(1)} collective-permute-done((f32[64,128]{1,0:T(8,128)S(1)}, f32[64,128]{1,0:T(8,128)S(1)}, u32[]{:S(2)}, u32[]{:S(2)}) %collective-permute-start.6) | collective-permute-done | bytes 32800 | tf_op jit(solution)/shard_map/ppermute | solution.py:245
  58.4 0.6 collective-permute-done.7
  59.0 2.7 %collective-permute-done.8 = f32[64,128]{1,0:T(8,128)S(1)} collective-permute-done((f32[64,128]{1,0:T(8,128)S(1)}, f32[64,128]{1,0:T(8,128)S(1)}, u32[]{:S(2)}, u32[]{:S(2)}) %collective-permute-start.8) | collective-permute-done | bytes 32800 | tf_op jit(solution)/shard_map/ppermute | solution.py:245
  61.6 0.6 %fusion.1 = f32[64,128]{1,0:T(8,128)} fusion(f32[64,128]{1,0:T(8,128)S(1)} %collective-permute-done.8, f32[64,128]{1,0:T(8,128)S(1)} %collective-permute-done.7, f32[64,128]{1,0:T(8,128)S(1)} %collective-permute-done.6, f32[256,128]{1,0:T(8,128)S(1)} %add.12), kind=kLoop, calls=%fused_computation.2 | loop fusion | flops 24576 | bytes 163840 | tf_op jit(solution)/shard_map/add | solution.py:246
  (3 shorter events, 0.0 us)
Async XLA Ops:
  1.7 7.2 %copy-start.1 = (f32[8,128]{1,0:T(8,128)S(1)}, f32[8,128]{1,0:T(8,128)}, u32[]{:S(2)}) copy-start(f32[8,128]{1,0:T(8,128)} %get-tuple-element.19) | copy-start | bytes 12292
  1.7 23.0 %copy-start = (f32[128,128]{1,0:T(8,128)S(1)}, f32[128,128]{1,0:T(8,128)}, u32[]{:S(2)}) copy-start(f32[128,128]{1,0:T(8,128)} %get-tuple-element.21.refs_5_.ports) | copy-start | bytes 196612
  1.7 22.0 %all-to-all-start = ((f32[16,72,128]{2,1,0:T(8,128)}), f32[16,72,128]{2,1,0:T(8,128)S(1)}, u32[]{:S(2)}, u32[]{:S(2)}) async-start(f32[16,72,128]{2,1,0:T(8,128)} %get-tuple-element.18), calls=%async_computation | async-start | bytes 1179648 | tf_op jit(solution)/shard_map/all_to_all | solution.py:234
  8.9 1.3 %collective-permute-start = (f32[8,128]{1,0:T(8,128)S(1)}, f32[8,128]{1,0:T(8,128)S(1)}, u32[]{:S(2)}, u32[]{:S(2)}) collective-permute-start(f32[8,128]{1,0:T(8,128)S(1)} %copy-done.1), channel_id=1, source_target_pairs={{0,1},{1,0},{2,3},{3,2},{4,5},{5,4},{6,7},{7,6},{8,9},{9,8},{10,11... | collective-permute-start | bytes 12296 | tf_op jit(solution)/shard_map/ppermute | solution.py:233
  10.1 7.9 %collective-permute-start.1 = (f32[2,8,128]{2,1,0:T(8,128)S(1)}, f32[2,8,128]{2,1,0:T(8,128)S(1)}, u32[]{:S(2)}, u32[]{:S(2)}) collective-permute-start(f32[2,8,128]{2,1,0:T(8,128)S(1)} %pad_maximum_fusion.refs_0_), channel_id=1, source_target_pairs={{0,8},{4,12},{8,0},{12,4},{1,9},{5,13},{9,1},{13,5},{2,10},{6,14},... | collective-permute-start | bytes 24584 | tf_op jit(solution)/shard_map/ppermute | solution.py:237
  16.4 4.5 %collective-permute-start.2 = (f32[2,8,128]{2,1,0:T(8,128)S(1)}, f32[2,8,128]{2,1,0:T(8,128)S(1)}, u32[]{:S(2)}, u32[]{:S(2)}) collective-permute-start(f32[2,8,128]{2,1,0:T(8,128)S(1)} %pad_maximum_fusion.refs_0_), channel_id=1, source_target_pairs={{0,4},{4,0},{8,12},{12,8},{1,5},{5,1},{9,13},{13,9},{2,6},{6,2},{1... | collective-permute-start | bytes 24584 | tf_op jit(solution)/shard_map/ppermute | solution.py:237
  17.9 5.8 %collective-permute-start.3 = (f32[2,8,128]{2,1,0:T(8,128)S(1)}, f32[2,8,128]{2,1,0:T(8,128)S(1)}, u32[]{:S(2)}, u32[]{:S(2)}) collective-permute-start(f32[2,8,128]{2,1,0:T(8,128)S(1)} %pad_maximum_fusion.refs_0_), channel_id=1, source_target_pairs={{0,12},{4,8},{8,4},{12,0},{1,13},{5,9},{9,5},{13,1},{2,14},{6,10},... | collective-permute-start | bytes 24584 | tf_op jit(solution)/shard_map/ppermute | solution.py:237
  23.7 13.7 %collective-permute-start.4 = (f32[16,72,128]{2,1,0:T(8,128)S(1)}, f32[16,72,128]{2,1,0:T(8,128)S(1)}, u32[]{:S(2)}, u32[]{:S(2)}) collective-permute-start(f32[16,72,128]{2,1,0:T(8,128)S(1)} %all-to-all-done.refs_4_), channel_id=1, source_target_pairs={{0,2},{2,0},{1,3},{3,1},{4,6},{6,4},{5,7},{7,5},{8,10},{10,8},{9,1... | collective-permute-start | bytes 1769480 | tf_op jit(solution)/shard_map/ppermute | solution.py:239
  48.9 1.4 %collective-permute-start.5 = (f32[256,128]{1,0:T(8,128)S(1)}, f32[256,128]{1,0:T(8,128)S(1)}, u32[]{:S(2)}, u32[]{:S(2)}) collective-permute-start(f32[256,128]{1,0:T(8,128)S(1)} %get-tuple-element.30), channel_id=1, source_target_pairs={{0,1},{1,0},{2,3},{3,2},{4,5},{5,4},{6,7},{7,6},{8,9},{9,8},{10,11... | collective-permute-start | bytes 393224 | tf_op jit(solution)/shard_map/ppermute | solution.py:242
  50.4 8.0 %collective-permute-start.6 = (f32[64,128]{1,0:T(8,128)S(1)}, f32[64,128]{1,0:T(8,128)S(1)}, u32[]{:S(2)}, u32[]{:S(2)}) collective-permute-start(f32[64,128]{1,0:T(8,128)S(1)} %get-tuple-element.31), channel_id=1, source_target_pairs={{0,8},{4,12},{8,0},{12,4},{1,9},{5,13},{9,1},{13,5},{2,10},{6,14},... | collective-permute-start | bytes 98312 | tf_op jit(solution)/shard_map/ppermute | solution.py:245
  54.1 4.8 %collective-permute-start.7 = (f32[64,128]{1,0:T(8,128)S(1)}, f32[64,128]{1,0:T(8,128)S(1)}, u32[]{:S(2)}, u32[]{:S(2)}) collective-permute-start(f32[64,128]{1,0:T(8,128)S(1)} %get-tuple-element.33), channel_id=1, source_target_pairs={{0,4},{4,0},{8,12},{12,8},{1,5},{5,1},{9,13},{13,9},{2,6},{6,2},{1... | collective-permute-start | bytes 98312 | tf_op jit(solution)/shard_map/ppermute | solution.py:245
  55.6 6.0 %collective-permute-start.8 = (f32[64,128]{1,0:T(8,128)S(1)}, f32[64,128]{1,0:T(8,128)S(1)}, u32[]{:S(2)}, u32[]{:S(2)}) collective-permute-start(f32[64,128]{1,0:T(8,128)S(1)} %get-tuple-element.32), channel_id=1, source_target_pairs={{0,12},{4,8},{8,4},{12,0},{1,13},{5,9},{9,5},{13,1},{2,14},{6,10},... | collective-permute-start | bytes 98312 | tf_op jit(solution)/shard_map/ppermute | solution.py:245

commit v4 on v2

--- a/solution.py
+++ b/solution.py
@@ -8,7 +8,7 @@
 BF16 = jnp.bfloat16
 F32 = jnp.float32
 TILE = 256
-UNROLL = 8
+UNROLL = 16
 DEPTH = 32
 LANES = 128
 MIDDLE = 2.0

time: 62.9 us -> 62.9 us (level)
  no operation moved by 1% of the time
where the time goes in v4:
time: 62.9 us; the launch traced here: 62.2 us
  Pallas kernels  25 us (40%)
  starting transfers between devices  22.7 us (36%)
  waiting for transfers between devices  13.8 us (22%)
  other arithmetic  0.64 us (1%)
    pallas_call x1, Pallas kernels, near_volts(): pl.pallas_call(near_kernel, out_shape=[jax.ShapeDtypeStruct((ROWS, DEPTH)...  11.8 us
    pallas_call x1, Pallas kernels, far_volts(): pl.pallas_call(far_kernel, out_shape=[jax.ShapeDtypeStruct((ROWS // 2, LA...  11.5 us
    ppermute x3, starting transfers between devices, per_device(): lax.ppermute(pair, 'zh', [(i, i ^ k) for i in zh])  7.77 us
    all_to_all x1, starting transfers between devices, per_device(): sources = lax.all_to_all(copies, ('y', 'x'), 0, 0, tiled=True)  7.17 us
    ppermute x3, starting transfers between devices, per_device(): shares.append(lax.ppermute(partial[j], 'zh', [(i, i ^ k) for i in zh]))  6.58 us
    ppermute x3, waiting for transfers between devices, per_device(): lax.ppermute(pair, 'zh', [(i, i ^ k) for i in zh])  5.76 us
    ppermute x3, waiting for transfers between devices, per_device(): shares.append(lax.ppermute(partial[j], 'zh', [(i, i ^ k) for i in zh]))  4.65 us
    pallas_call x1, Pallas kernels, pack(): pl.pallas_call(pack_kernel, out_shape=[jax.ShapeDtypeStruct(shape, F32) f...  1.7 us
  transfers between devices with their start and end apart: 10, of which 9 were waited for; matrix products, arithmetic and copies ran while one was open for 0% of the time, Pallas kernels for 19%

profile of v4, /device:TPU:32, one launch (start us, length us, event | category | flops | bytes accessed | tf_op | source)
XLA Modules:
  0.0 62.2 jit_solution(7406547887775344669)
XLA Ops:
  0.0 1.7 %pack.1 = (f32[8,128]{1,0:T(8,128)}, f32[16,72,128]{2,1,0:T(8,128)}, f32[128,128]{1,0:T(8,128)}) custom-call(f32[3,64]{1,0:T(4,128)} %t_position.1, f32[3,64]{1,0:T(4,128)} %t_vector.1, f32[1,64]{1,0:T(1,128)} %bitcast.12, f32[3,1024]{1,0:T(4,128)} %refs_0_.1, f32[3,1024]{1,0:T(4,128)} %refs_1_.1, f32[8,128]{1,0:T(8,128)} %bitcast.7, f32[8,128]{1,0:T(8,128)} %bitcast.8, ...), custom_call_target="tpu_custom_call" | custom-call | tf_op jit(solution)/shard_map/pack/pallas_call | solution.py:84
  1.7 0.0 copy-start.1
  1.7 0.0 copy-start
  1.7 7.2 %all-to-all-start = ((f32[16,72,128]{2,1,0:T(8,128)}), f32[16,72,128]{2,1,0:T(8,128)S(1)}, u32[]{:S(2)}, u32[]{:S(2)}) async-start(f32[16,72,128]{2,1,0:T(8,128)} %get-tuple-element.18), calls=%async_computation | async-start | bytes 1179648 | tf_op jit(solution)/shard_map/all_to_all | solution.py:232
  8.9 0.0 copy-done.1
  8.9 0.1 collective-permute-start
  9.0 1.2 %collective-permute-done = f32[8,128]{1,0:T(8,128)S(1)} collective-permute-done((f32[8,128]{1,0:T(8,128)S(1)}, f32[8,128]{1,0:T(8,128)S(1)}, u32[]{:S(2)}, u32[]{:S(2)}) %collective-permute-start) | collective-permute-done | bytes 4128 | tf_op jit(solution)/shard_map/ppermute | solution.py:231
  10.1 6.3 %collective-permute-start.1 = (f32[2,8,128]{2,1,0:T(8,128)S(1)}, f32[2,8,128]{2,1,0:T(8,128)S(1)}, u32[]{:S(2)}, u32[]{:S(2)}) collective-permute-start(f32[2,8,128]{2,1,0:T(8,128)S(1)} %pad_maximum_fusion.refs_0_), channel_id=1, source_target_pairs={{0,8},{4,12},{8,0},{12,4},{1,9},{5,13},{9,1},{13,5},{2,10},{6,14},... | collective-permute-start | bytes 24584 | tf_op jit(solution)/shard_map/ppermute | solution.py:235
  16.4 1.5 %collective-permute-start.2 = (f32[2,8,128]{2,1,0:T(8,128)S(1)}, f32[2,8,128]{2,1,0:T(8,128)S(1)}, u32[]{:S(2)}, u32[]{:S(2)}) collective-permute-start(f32[2,8,128]{2,1,0:T(8,128)S(1)} %pad_maximum_fusion.refs_0_), channel_id=1, source_target_pairs={{0,4},{4,0},{8,12},{12,8},{1,5},{5,1},{9,13},{13,9},{2,6},{6,2},{1... | collective-permute-start | bytes 24584 | tf_op jit(solution)/shard_map/ppermute | solution.py:235
  17.9 0.0 collective-permute-start.3
  17.9 0.2 collective-permute-done.1.refs_1_
  18.1 2.9 %collective-permute-done.2.refs_2_ = f32[2,8,128]{2,1,0:T(8,128)S(1)} collective-permute-done((f32[2,8,128]{2,1,0:T(8,128)S(1)}, f32[2,8,128]{2,1,0:T(8,128)S(1)}, u32[]{:S(2)}, u32[]{:S(2)}) %collective-permute-start.2) | collective-permute-done | bytes 8224 | tf_op jit(solution)/shard_map/ppermute | solution.py:235
  21.0 2.7 %collective-permute-done.3.refs_3_ = f32[2,8,128]{2,1,0:T(8,128)S(1)} collective-permute-done((f32[2,8,128]{2,1,0:T(8,128)S(1)}, f32[2,8,128]{2,1,0:T(8,128)S(1)}, u32[]{:S(2)}, u32[]{:S(2)}) %collective-permute-start.3) | collective-permute-done | bytes 8224 | tf_op jit(solution)/shard_map/ppermute | solution.py:235
  23.7 0.0 all-to-all-done.refs_4_
  23.7 1.0 %collective-permute-start.4 = (f32[16,72,128]{2,1,0:T(8,128)S(1)}, f32[16,72,128]{2,1,0:T(8,128)S(1)}, u32[]{:S(2)}, u32[]{:S(2)}) collective-permute-start(f32[16,72,128]{2,1,0:T(8,128)S(1)} %all-to-all-done.refs_4_), channel_id=1, source_target_pairs={{0,2},{2,0},{1,3},{3,1},{4,6},{6,4},{5,7},{7,5},{8,10},{10,8},{9,1... | collective-permute-start | bytes 1769480 | tf_op jit(solution)/shard_map/ppermute | solution.py:237
  24.7 0.0 copy-done
  24.7 11.8 %near_volts.1 = (bf16[512,32]{1,0:T(8,128)(2,1)S(1)}, f32[3,512,128]{2,1,0:T(8,128)S(1)}, f32[512,128]{1,0:T(8,128)S(1)}) custom-call(f32[2,8,128]{2,1,0:T(8,128)S(1)} %pad_maximum_fusion.refs_0_, f32[2,8,128]{2,1,0:T(8,128)S(1)} %collective-permute-done.1.refs_1_, f32[2,8,128]{2,1,0:T(8,128)S(1)} %collective-permute-done.2.refs_2_, ...), custom_call_target="tpu_custom_call" | custom-call | flops 2684354560 | bytes 2097152 | tf_op jit(solution)/shard_map/near_volts/pallas_call | solution.py:178
  36.5 0.9 %collective-permute-done.4.sources = f32[16,72,128]{2,1,0:T(8,128)S(1)} collective-permute-done((f32[16,72,128]{2,1,0:T(8,128)S(1)}, f32[16,72,128]{2,1,0:T(8,128)S(1)}, u32[]{:S(2)}, u32[]{:S(2)}) %collective-permute-start.4) | collective-permute-done | bytes 589856 | tf_op jit(solution)/shard_map/ppermute | solution.py:237
  37.4 11.5 %far_volts.1 = (f32[256,128]{1,0:T(8,128)S(1)}, f32[256,128]{1,0:T(8,128)S(1)}) custom-call(f32[16,72,128]{2,1,0:T(8,128)S(1)} %collective-permute-done.4.sources, f32[128,128]{1,0:T(8,128)S(1)} %copy-done, bf16[512,32]{1,0:T(8,128)(2,1)S(1)} %get-tuple-element.26.squared, f32[3,512,128]{2,1,0:T(8,128)S(1)} %get-tuple-element.27.vectors, ...), custom_call_target="tpu_custom_call" | custom-call | flops 2684354560 | bytes 2097152 | tf_op jit(solution)/shard_map/far_volts/pallas_call | solution.py:195
  48.9 0.1 collective-permute-start.5
  49.0 1.3 %collective-permute-done.5 = f32[256,128]{1,0:T(8,128)S(1)} collective-permute-done((f32[256,128]{1,0:T(8,128)S(1)}, f32[256,128]{1,0:T(8,128)S(1)}, u32[]{:S(2)}, u32[]{:S(2)}) %collective-permute-start.5) | collective-permute-done | bytes 131104 | tf_op jit(solution)/shard_map/ppermute | solution.py:240
  50.4 3.7 %collective-permute-start.6 = (f32[64,128]{1,0:T(8,128)S(1)}, f32[64,128]{1,0:T(8,128)S(1)}, u32[]{:S(2)}, u32[]{:S(2)}) collective-permute-start(f32[64,128]{1,0:T(8,128)S(1)} %get-tuple-element.31), channel_id=1, source_target_pairs={{0,8},{4,12},{8,0},{12,4},{1,9},{5,13},{9,1},{13,5},{2,10},{6,14},... | collective-permute-start | bytes 98312 | tf_op jit(solution)/shard_map/ppermute | solution.py:243
  54.1 1.5 %collective-permute-start.7 = (f32[64,128]{1,0:T(8,128)S(1)}, f32[64,128]{1,0:T(8,128)S(1)}, u32[]{:S(2)}, u32[]{:S(2)}) collective-permute-start(f32[64,128]{1,0:T(8,128)S(1)} %get-tuple-element.33), channel_id=1, source_target_pairs={{0,4},{4,0},{8,12},{12,8},{1,5},{5,1},{9,13},{13,9},{2,6},{6,2},{1... | collective-permute-start | bytes 98312 | tf_op jit(solution)/shard_map/ppermute | solution.py:243
  55.6 1.4 %collective-permute-start.8 = (f32[64,128]{1,0:T(8,128)S(1)}, f32[64,128]{1,0:T(8,128)S(1)}, u32[]{:S(2)}, u32[]{:S(2)}) collective-permute-start(f32[64,128]{1,0:T(8,128)S(1)} %get-tuple-element.32), channel_id=1, source_target_pairs={{0,12},{4,8},{8,4},{12,0},{1,13},{5,9},{9,5},{13,1},{2,14},{6,10},... | collective-permute-start | bytes 98312 | tf_op jit(solution)/shard_map/ppermute | solution.py:243
  57.0 1.4 %collective-permute-done.6 = f32[64,128]{1,0:T(8,128)S(1)} collective-permute-done((f32[64,128]{1,0:T(8,128)S(1)}, f32[64,128]{1,0:T(8,128)S(1)}, u32[]{:S(2)}, u32[]{:S(2)}) %collective-permute-start.6) | collective-permute-done | bytes 32800 | tf_op jit(solution)/shard_map/ppermute | solution.py:243
  58.4 0.6 collective-permute-done.7
  59.0 2.6 %collective-permute-done.8 = f32[64,128]{1,0:T(8,128)S(1)} collective-permute-done((f32[64,128]{1,0:T(8,128)S(1)}, f32[64,128]{1,0:T(8,128)S(1)}, u32[]{:S(2)}, u32[]{:S(2)}) %collective-permute-start.8) | collective-permute-done | bytes 32800 | tf_op jit(solution)/shard_map/ppermute | solution.py:243
  61.6 0.6 %fusion.1 = f32[64,128]{1,0:T(8,128)} fusion(f32[64,128]{1,0:T(8,128)S(1)} %collective-permute-done.8, f32[64,128]{1,0:T(8,128)S(1)} %collective-permute-done.7, f32[64,128]{1,0:T(8,128)S(1)} %collective-permute-done.6, f32[256,128]{1,0:T(8,128)S(1)} %add.12), kind=kLoop, calls=%fused_computation.2 | loop fusion | flops 24576 | bytes 163840 | tf_op jit(solution)/shard_map/add | solution.py:244
  (3 shorter events, 0.0 us)
Async XLA Ops:
  1.7 7.2 %copy-start.1 = (f32[8,128]{1,0:T(8,128)S(1)}, f32[8,128]{1,0:T(8,128)}, u32[]{:S(2)}) copy-start(f32[8,128]{1,0:T(8,128)} %get-tuple-element.19) | copy-start | bytes 12292
  1.7 23.0 %copy-start = (f32[128,128]{1,0:T(8,128)S(1)}, f32[128,128]{1,0:T(8,128)}, u32[]{:S(2)}) copy-start(f32[128,128]{1,0:T(8,128)} %get-tuple-element.21.refs_5_.ports) | copy-start | bytes 196612
  1.7 22.0 %all-to-all-start = ((f32[16,72,128]{2,1,0:T(8,128)}), f32[16,72,128]{2,1,0:T(8,128)S(1)}, u32[]{:S(2)}, u32[]{:S(2)}) async-start(f32[16,72,128]{2,1,0:T(8,128)} %get-tuple-element.18), calls=%async_computation | async-start | bytes 1179648 | tf_op jit(solution)/shard_map/all_to_all | solution.py:232
  8.9 1.3 %collective-permute-start = (f32[8,128]{1,0:T(8,128)S(1)}, f32[8,128]{1,0:T(8,128)S(1)}, u32[]{:S(2)}, u32[]{:S(2)}) collective-permute-start(f32[8,128]{1,0:T(8,128)S(1)} %copy-done.1), channel_id=1, source_target_pairs={{0,1},{1,0},{2,3},{3,2},{4,5},{5,4},{6,7},{7,6},{8,9},{9,8},{10,11... | collective-permute-start | bytes 12296 | tf_op jit(solution)/shard_map/ppermute | solution.py:231
  10.1 7.9 %collective-permute-start.1 = (f32[2,8,128]{2,1,0:T(8,128)S(1)}, f32[2,8,128]{2,1,0:T(8,128)S(1)}, u32[]{:S(2)}, u32[]{:S(2)}) collective-permute-start(f32[2,8,128]{2,1,0:T(8,128)S(1)} %pad_maximum_fusion.refs_0_), channel_id=1, source_target_pairs={{0,8},{4,12},{8,0},{12,4},{1,9},{5,13},{9,1},{13,5},{2,10},{6,14},... | collective-permute-start | bytes 24584 | tf_op jit(solution)/shard_map/ppermute | solution.py:235
  16.4 4.5 %collective-permute-start.2 = (f32[2,8,128]{2,1,0:T(8,128)S(1)}, f32[2,8,128]{2,1,0:T(8,128)S(1)}, u32[]{:S(2)}, u32[]{:S(2)}) collective-permute-start(f32[2,8,128]{2,1,0:T(8,128)S(1)} %pad_maximum_fusion.refs_0_), channel_id=1, source_target_pairs={{0,4},{4,0},{8,12},{12,8},{1,5},{5,1},{9,13},{13,9},{2,6},{6,2},{1... | collective-permute-start | bytes 24584 | tf_op jit(solution)/shard_map/ppermute | solution.py:235
  17.9 5.8 %collective-permute-start.3 = (f32[2,8,128]{2,1,0:T(8,128)S(1)}, f32[2,8,128]{2,1,0:T(8,128)S(1)}, u32[]{:S(2)}, u32[]{:S(2)}) collective-permute-start(f32[2,8,128]{2,1,0:T(8,128)S(1)} %pad_maximum_fusion.refs_0_), channel_id=1, source_target_pairs={{0,12},{4,8},{8,4},{12,0},{1,13},{5,9},{9,5},{13,1},{2,14},{6,10},... | collective-permute-start | bytes 24584 | tf_op jit(solution)/shard_map/ppermute | solution.py:235
  23.7 13.7 %collective-permute-start.4 = (f32[16,72,128]{2,1,0:T(8,128)S(1)}, f32[16,72,128]{2,1,0:T(8,128)S(1)}, u32[]{:S(2)}, u32[]{:S(2)}) collective-permute-start(f32[16,72,128]{2,1,0:T(8,128)S(1)} %all-to-all-done.refs_4_), channel_id=1, source_target_pairs={{0,2},{2,0},{1,3},{3,1},{4,6},{6,4},{5,7},{7,5},{8,10},{10,8},{9,1... | collective-permute-start | bytes 1769480 | tf_op jit(solution)/shard_map/ppermute | solution.py:237
  48.9 1.4 %collective-permute-start.5 = (f32[256,128]{1,0:T(8,128)S(1)}, f32[256,128]{1,0:T(8,128)S(1)}, u32[]{:S(2)}, u32[]{:S(2)}) collective-permute-start(f32[256,128]{1,0:T(8,128)S(1)} %get-tuple-element.30), channel_id=1, source_target_pairs={{0,1},{1,0},{2,3},{3,2},{4,5},{5,4},{6,7},{7,6},{8,9},{9,8},{10,11... | collective-permute-start | bytes 393224 | tf_op jit(solution)/shard_map/ppermute | solution.py:240
  50.4 8.0 %collective-permute-start.6 = (f32[64,128]{1,0:T(8,128)S(1)}, f32[64,128]{1,0:T(8,128)S(1)}, u32[]{:S(2)}, u32[]{:S(2)}) collective-permute-start(f32[64,128]{1,0:T(8,128)S(1)} %get-tuple-element.31), channel_id=1, source_target_pairs={{0,8},{4,12},{8,0},{12,4},{1,9},{5,13},{9,1},{13,5},{2,10},{6,14},... | collective-permute-start | bytes 98312 | tf_op jit(solution)/shard_map/ppermute | solution.py:243
  54.1 4.8 %collective-permute-start.7 = (f32[64,128]{1,0:T(8,128)S(1)}, f32[64,128]{1,0:T(8,128)S(1)}, u32[]{:S(2)}, u32[]{:S(2)}) collective-permute-start(f32[64,128]{1,0:T(8,128)S(1)} %get-tuple-element.33), channel_id=1, source_target_pairs={{0,4},{4,0},{8,12},{12,8},{1,5},{5,1},{9,13},{13,9},{2,6},{6,2},{1... | collective-permute-start | bytes 98312 | tf_op jit(solution)/shard_map/ppermute | solution.py:243
  55.6 6.0 %collective-permute-start.8 = (f32[64,128]{1,0:T(8,128)S(1)}, f32[64,128]{1,0:T(8,128)S(1)}, u32[]{:S(2)}, u32[]{:S(2)}) collective-permute-start(f32[64,128]{1,0:T(8,128)S(1)} %get-tuple-element.32), channel_id=1, source_target_pairs={{0,12},{4,8},{8,4},{12,0},{1,13},{5,9},{9,5},{13,1},{2,14},{6,10},... | collective-permute-start | bytes 98312 | tf_op jit(solution)/shard_map/ppermute | solution.py:243
